TPU v7x, 256 devices: a whole 4x4x8 slice. The times are simulated.
256 devices in a mesh: row: 4 (over x), col: 8 (over y, core), layer: 8 (over z).
Axes of the slice: x: 4, y: 4, z: 8, core: 2. Of those that a mesh axis runs over, the one named last changes fastest.
Arguments:
- blocks: float32 [128, 16, 128, 128], P(('row', 'col'), 'layer'), as said below
- columns: int32 [128, 16], replicated, may hold values from -1 to 127, as said below
- signs: int32 [3], replicated, may hold values from 0 to 1, as said below
Outputs:
- purified: float32 [128, 16, 128, 128], P(('row', 'col'), 'layer')
- traces: float32 [3], replicated
Inputs may be any that keep to these rules, and one draw needn't show every extreme that they name: Slots l * 2 to (l + 1) * 2 - 1 of row i hold, in increasing order and then padded with -1, the block columns j of row i's pattern with j % 8 = l. Every j satisfies |i - j| <= 4. The pattern is symmetric and holds every j with |i - j| <= 1 or |i - j| = 4. blocks[i, q] is the block (i, columns[i, q]) of a symmetric matrix: block (j, i) is the transpose of block (i, j). Empty slots hold zeros. `signs`: both branches occur among the 3 steps.
All inputs are finite; a program needn't handle non-finite values.
Results may differ from a plain program's by a relative error of at most 0.0003.
Values sent between devices are 32-bit elements; how exact they have to be, the bound alone decides.
A program may use at most 128 MiB of HBM per device.

v0:
```python
import jax
import jax.numpy as jnp
from jax import lax
from jax.sharding import PartitionSpec as P

NEAR = 4
ITERS = 3


def with_halo(value, sides, width):
    for axis, dim in sides:
        peers, length = (lax.axis_size(axis), value.shape[dim])
        up = [(i, (i + 1) % peers) for i in range(peers - 1)]
        down = [(j, i) for i, j in up]
        last = lax.slice_in_dim(value, length - width, length, axis=dim)
        initial = lax.slice_in_dim(value, 0, width, axis=dim)
        before = lax.ppermute(last, axis, up)
        after = lax.ppermute(initial, axis, down)
        value = jnp.concatenate([before, value, after], axis=dim)
    return value


def band_of(rows, row_cols, first_row):
    height = rows.shape[0]
    reach = jnp.arange(-NEAR, NEAR + 1, dtype=jnp.int32)
    wanted = first_row + jnp.arange(height, dtype=jnp.int32)[:, None] + reach[None, :]
    onehot = ((row_cols[:, None, :] == wanted[:, :, None]) & (row_cols[:, None, :] >= 0)).astype(
        jnp.float32
    )
    return jnp.einsum("hds,hsab->hdab", onehot, rows, precision=lax.Precision.HIGHEST)


def pair_products(band, near_base, own_cols, row_start):
    height = band.shape[0]
    reach = jnp.arange(-NEAR, NEAR + 1, dtype=jnp.int32)

    def one_row(offset):
        row_id = row_start + offset
        own = lax.dynamic_index_in_dim(band, row_id - near_base, 0, keepdims=False)
        targets = lax.dynamic_index_in_dim(own_cols, offset, 0, keepdims=False)
        local = jnp.clip(targets - near_base, 0, height - 1)
        moved = reach[None, :] - (targets - row_id)[:, None]
        valid = (jnp.abs(moved) <= NEAR) & (targets >= 0)[:, None]
        partner = band[local[:, None], jnp.clip(moved + NEAR, 0, 2 * NEAR)]
        partner = jnp.where(valid[:, :, None, None], partner, jnp.float32(0.0))
        result = jnp.einsum("dac,qdbc->qab", own, partner, precision=lax.Precision.HIGHEST)
        return jnp.where((targets >= 0)[:, None, None], result, jnp.float32(0.0))

    return lax.map(one_row, jnp.arange(own_cols.shape[0], dtype=jnp.int32))


def shards(blocks, columns, signs):
    slab_index = lax.axis_index("layer")
    row_total = blocks.shape[0]
    slot_width = blocks.shape[1]
    row_start = lax.axis_index(("row", "col")) * row_total
    orbitals = row_total * lax.axis_size(("row", "col")) * blocks.shape[2]
    padded_cols = jnp.pad(columns, ((NEAR, NEAR), (0, 0)), constant_values=-1)
    window_cols = lax.dynamic_slice_in_dim(padded_cols, row_start, row_total + 2 * NEAR, 0)
    near_base = row_start - NEAR
    own_rows_cols = lax.dynamic_slice_in_dim(columns, row_start, row_total, 0)
    slab_cols = lax.dynamic_slice_in_dim(own_rows_cols, slab_index * slot_width, slot_width, 1)
    is_diag = slab_cols == (row_start + jnp.arange(row_total, dtype=jnp.int32))[:, None]
    current = blocks
    local_traces = []
    for iteration in range(ITERS):
        whole_rows = lax.all_gather(current, "layer", axis=1, tiled=True)
        nearby = with_halo(whole_rows, ((("row", "col"), 0),), NEAR)
        band = band_of(nearby, window_cols, near_base)
        squared = pair_products(band, near_base, slab_cols, row_start)
        current = jnp.where(signs[iteration] == 1, squared, 2.0 * current - squared)
        diag_trace = jnp.sum(
            jnp.where(is_diag, jnp.trace(current, axis1=2, axis2=3), jnp.float32(0.0))
        )
        local_traces.append(lax.psum(diag_trace, ("row", "col", "layer")))
    stacked = jnp.stack(local_traces)
    return (current, stacked / orbitals)


def solution(mesh):
    return jax.shard_map(
        shards,
        mesh=mesh,
        in_specs=(P(("row", "col"), "layer", None, None), P(), P()),
        out_specs=(P(("row", "col"), "layer", None, None), P()),
        check_vma=False,
    )
```

profile of v0, /device:TPU:1, one launch (start us, length us, event | category | flops | bytes accessed | tf_op | source)
XLA Modules:
  0.0 605.9 jit_solution(5223474772262809516)
XLA Ops:
  9.2 59.8 %all-gather.4.cloned.1.call-done = f32[4,16,128,128]{3,2,0,1:T(8,128)} async-done(((f32[4,2,128,128]{3,2,0,1:T(8,128)}), f32[4,16,128,128]{3,2,0,1:T(8,128)}) %all-gather.4.cloned.1.call-update) | async-done | bytes 4194320 | tf_op jit(solution)/shard_map/all_gather | solution.py:67
  69.0 6.6 %copy.53 = f32[4,16,128,128]{3,1,2,0:T(8,128)} copy(f32[4,16,128,128]{3,2,0,1:T(8,128)} %all-gather.4.cloned.1.call-done) | data formatting | bytes 8388608 | tf_op jit(solution)/shard_map/all_gather | solution.py:67
  75.6 3.7 collective-permute-start
  83.7 41.3 %collective-permute-done = f32[4,16,128,128]{3,1,2,0:T(8,128)} collective-permute-done((f32[4,16,128,128]{3,1,2,0:T(8,128)}, f32[4,16,128,128]{3,1,2,0:T(8,128)}, u32[]{:S(2)}, u32[]{:S(2)}) %collective-permute-start) | collective-permute-done | bytes 4194336 | tf_op jit(solution)/shard_map/ppermute | solution.py:17
  125.0 4.4 collective-permute-done.1
  129.4 9.3 %fusion.72 = f32[12,9,128,128]{3,1,2,0:T(8,128)S(1)} fusion(f32[4,16,128,128]{3,1,2,0:T(8,128)} %collective-permute-done.1, f32[4,16,128,128]{3,1,2,0:T(8,128)} %copy.53, f32[4,16,128,128]{3,1,2,0:T(8,128)} %collective-permute-done, s32[12,9]{1,0:T(8,128)S(1)} %broadcast_add_fusion, s32[12,16]{1,0:T(8,128)S(1)} %copy.50, pred[12,16]{1,0:T(8,128)(4,1)S(1)} %copy.51), kind=kOutput, calls=%fused_computation.78 | convolution fusion | flops 346033536 | bytes 19662192 | tf_op jit(solution)/shard_map/hds,hsab->hdab/dot_general | solution.py:30
  138.7 5.1 copy.58
  143.8 38.1 %while.36 = (s32[]{:T(128)}, f32[4,2,128,128]{3,2,0,1:T(8,128)S(1)}, s32[4]{0:T(128)S(1)}, s32[4,2]{1,0:T(4,128)S(1)}, s32[]{:T(128)}, /*index=5*/s32[]{:T(128)}...) while((s32[]{:T(128)}, ...), condition=%wide.region_1.2_spmd.clone.clone, body=%wide.region_0.1_spmd.clone.clone.sunk | while | flops 453312768 | bytes 4784943 | solution.py:49
  183.0 54.3 %all-gather.6.cloned.1.call-done = f32[4,16,128,128]{3,2,0,1:T(8,128)} async-done(((f32[4,2,128,128]{3,2,0,1:T(8,128)}), f32[4,16,128,128]{3,2,0,1:T(8,128)}) %all-gather.6.cloned.1.call-update) | async-done | bytes 4194320 | tf_op jit(solution)/shard_map/all_gather | solution.py:67
  237.2 6.6 %copy.62 = f32[4,16,128,128]{3,1,2,0:T(8,128)} copy(f32[4,16,128,128]{3,2,0,1:T(8,128)} %all-gather.6.cloned.1.call-done) | data formatting | bytes 8388608 | tf_op jit(solution)/shard_map/all_gather | solution.py:67
  243.8 3.7 collective-permute-start.2
  250.7 42.5 %collective-permute-done.2 = f32[4,16,128,128]{3,1,2,0:T(8,128)} collective-permute-done((f32[4,16,128,128]{3,1,2,0:T(8,128)}, f32[4,16,128,128]{3,1,2,0:T(8,128)}, u32[]{:S(2)}, u32[]{:S(2)}) %collective-permute-start.2) | collective-permute-done | bytes 4194336 | tf_op jit(solution)/shard_map/ppermute | solution.py:17
  293.2 4.4 collective-permute-done.3
  297.6 9.3 %fusion.78 = f32[12,9,128,128]{3,1,2,0:T(8,128)S(1)} fusion(f32[4,16,128,128]{3,1,2,0:T(8,128)} %collective-permute-done.3, f32[4,16,128,128]{3,1,2,0:T(8,128)} %copy.62, f32[4,16,128,128]{3,1,2,0:T(8,128)} %collective-permute-done.2, s32[12,9]{1,0:T(8,128)S(1)} %broadcast_add_fusion, s32[12,16]{1,0:T(8,128)S(1)} %copy.50, pred[12,16]{1,0:T(8,128)(4,1)S(1)} %copy.51), kind=kOutput, calls=%fused_computation.84 | convolution fusion | flops 346033536 | bytes 19662192 | tf_op jit(solution)/shard_map/hds,hsab->hdab/dot_general | solution.py:30
  306.9 5.1 copy.67
  312.0 37.6 %while.37 = (s32[]{:T(128)}, f32[4,2,128,128]{3,2,0,1:T(8,128)S(1)}, s32[4]{0:T(128)S(1)}, s32[4,2]{1,0:T(4,128)S(1)}, s32[]{:T(128)}, /*index=5*/s32[]{:T(128)}...) while((s32[]{:T(128)}, ...), condition=%wide.region_3.4_spmd.clone.clone, body=%wide.region_2.3_spmd.clone.clone.sunk | while | flops 453312768 | bytes 4784943 | solution.py:49
  350.5 54.5 %all-gather.8.cloned.1.call-done = f32[4,16,128,128]{3,2,0,1:T(8,128)} async-done(((f32[4,2,128,128]{3,2,0,1:T(8,128)}), f32[4,16,128,128]{3,2,0,1:T(8,128)}) %all-gather.8.cloned.1.call-update) | async-done | bytes 4194320 | tf_op jit(solution)/shard_map/all_gather | solution.py:67
  405.1 6.6 %copy.70 = f32[4,16,128,128]{3,1,2,0:T(8,128)} copy(f32[4,16,128,128]{3,2,0,1:T(8,128)} %all-gather.8.cloned.1.call-done) | data formatting | bytes 8388608 | tf_op jit(solution)/shard_map/all_gather | solution.py:67
  418.8 42.2 %collective-permute-done.4 = f32[4,16,128,128]{3,1,2,0:T(8,128)} collective-permute-done((f32[4,16,128,128]{3,1,2,0:T(8,128)}, f32[4,16,128,128]{3,1,2,0:T(8,128)}, u32[]{:S(2)}, u32[]{:S(2)}) %collective-permute-start.4) | collective-permute-done | bytes 4194336 | tf_op jit(solution)/shard_map/ppermute | solution.py:17
  461.0 4.4 collective-permute-done.5
  465.4 9.3 %fusion.84 = f32[12,9,128,128]{3,1,2,0:T(8,128)S(1)} fusion(f32[4,16,128,128]{3,1,2,0:T(8,128)} %collective-permute-done.5, f32[4,16,128,128]{3,1,2,0:T(8,128)} %copy.70, f32[4,16,128,128]{3,1,2,0:T(8,128)} %collective-permute-done.4, s32[12,9]{1,0:T(8,128)S(1)} %broadcast_add_fusion, s32[12,16]{1,0:T(8,128)S(1)} %copy.50, pred[12,16]{1,0:T(8,128)(4,1)S(1)} %copy.51), kind=kOutput, calls=%fused_computation.90 | convolution fusion | flops 346033536 | bytes 19662192 | tf_op jit(solution)/shard_map/hds,hsab->hdab/dot_general | solution.py:30
  474.7 5.1 copy.75
  479.8 38.0 %while.38 = (s32[]{:T(128)}, f32[4,2,128,128]{3,2,0,1:T(8,128)S(1)}, s32[4]{0:T(128)S(1)}, s32[4,2]{1,0:T(4,128)S(1)}, s32[]{:T(128)}, /*index=5*/s32[]{:T(128)}...) while((s32[]{:T(128)}, ...), condition=%wide.region_5.6_spmd.clone.clone, body=%wide.region_4.5_spmd.clone.clone.sunk | while | flops 453312768 | bytes 4784943 | solution.py:49
  519.6 77.4 %all-reduce.1 = (f32[1]{0:T(128)}, f32[1]{0:T(128)}, f32[1]{0:T(128)}) all-reduce(f32[1]{0:T(128)} %bitcast.8, f32[1]{0:T(128)} %bitcast.7, f32[1]{0:T(128)} %bitcast.6), channel_id=1, replica_groups=mesh['row'=4,'col'=8,'layer'=8] {'row','col','layer'}, use_global_device_ids=true, to_apply=%region_14.15 | all-reduce | flops 3 | bytes 24 | tf_op jit(solution)/shard_map/psum | solution.py:75
  (190 shorter events, 103.6 us)
Async XLA Ops:
  7.2 61.9 %all-gather.4.cloned.1.call-start = ((), (), s32[]{:S(2)}) async-start(), calls=%async_computation | async-start | bytes 4718592 | tf_op jit(solution)/shard_map/all_gather | solution.py:67
  9.1 72.8 %copy-start.4 = (s32[128,16]{0,1:T(8,128)S(1)}, s32[128,16]{0,1:T(8,128)}, u32[]{:S(2)}) copy-start(s32[128,16]{0,1:T(8,128)} %param.10) | copy-start | bytes 24580
  9.1 73.2 %copy-start.5 = (s32[3]{0:T(128)S(1)}, s32[3]{0:T(128)}, u32[]{:S(2)}) copy-start(s32[3]{0:T(128)} %param.11) | copy-start | bytes 40
  9.1 228.1 %all-gather.6.cloned.1.call-start = ((), (), s32[]{:S(2)}) async-start(), calls=%async_computation.1 | async-start | bytes 4718592 | tf_op jit(solution)/shard_map/all_gather | solution.py:67
  75.6 49.4 %collective-permute-start = (f32[4,16,128,128]{3,1,2,0:T(8,128)}, f32[4,16,128,128]{3,1,2,0:T(8,128)}, u32[]{:S(2)}, u32[]{:S(2)}) collective-permute-start(f32[4,16,128,128]{3,1,2,0:T(8,128)} %copy.53), channel_id=1, source_target_pairs={{0,8},{8,16},{16,24},{24,32},{32,40},{40,48},{48,56},{56,64},{64,7... | collective-permute-start | bytes 12582920 | tf_op jit(solution)/shard_map/ppermute | solution.py:17
  79.2 50.1 %collective-permute-start.1 = (f32[4,16,128,128]{3,1,2,0:T(8,128)}, f32[4,16,128,128]{3,1,2,0:T(8,128)}, u32[]{:S(2)}, u32[]{:S(2)}) collective-permute-start(f32[4,16,128,128]{3,1,2,0:T(8,128)} %copy.53), channel_id=1, source_target_pairs={{8,0},{16,8},{24,16},{32,24},{40,32},{48,40},{56,48},{64,56},{72,6... | collective-permute-start | bytes 12582920 | tf_op jit(solution)/shard_map/ppermute | solution.py:18
  143.7 38.1 %copy-start.3 = (f32[4,2,128,128]{3,2,1,0:T(8,128)S(1)}, f32[4,2,128,128]{3,2,1,0:T(8,128)}, u32[]{:S(2)}) copy-start(f32[4,2,128,128]{3,2,1,0:T(8,128)} %param.9) | copy-start | bytes 1572868
  182.7 222.3 %all-gather.8.cloned.1.call-start = ((), (), s32[]{:S(2)}) async-start(), calls=%async_computation.2 | async-start | bytes 4718592 | tf_op jit(solution)/shard_map/all_gather | solution.py:67
  243.8 49.4 %collective-permute-start.2 = (f32[4,16,128,128]{3,1,2,0:T(8,128)}, f32[4,16,128,128]{3,1,2,0:T(8,128)}, u32[]{:S(2)}, u32[]{:S(2)}) collective-permute-start(f32[4,16,128,128]{3,1,2,0:T(8,128)} %copy.62), channel_id=1, source_target_pairs={{0,8},{8,16},{16,24},{24,32},{32,40},{40,48},{48,56},{56,64},{64,7... | collective-permute-start | bytes 12582920 | tf_op jit(solution)/shard_map/ppermute | solution.py:17
  247.5 50.1 %collective-permute-start.3 = (f32[4,16,128,128]{3,1,2,0:T(8,128)}, f32[4,16,128,128]{3,1,2,0:T(8,128)}, u32[]{:S(2)}, u32[]{:S(2)}) collective-permute-start(f32[4,16,128,128]{3,1,2,0:T(8,128)} %copy.62), channel_id=1, source_target_pairs={{8,0},{16,8},{24,16},{32,24},{40,32},{48,40},{56,48},{64,56},{72,6... | collective-permute-start | bytes 12582920 | tf_op jit(solution)/shard_map/ppermute | solution.py:18
  312.0 37.6 %copy-start = (f32[4,2,128,128]{3,2,0,1:T(8,128)S(1)}, f32[4,2,128,128]{3,2,0,1:T(8,128)}, u32[]{:S(2)}) copy-start(f32[4,2,128,128]{3,2,0,1:T(8,128)} %subtract_select_fusion.2) | copy-start | bytes 1572868
  411.6 49.4 %collective-permute-start.4 = (f32[4,16,128,128]{3,1,2,0:T(8,128)}, f32[4,16,128,128]{3,1,2,0:T(8,128)}, u32[]{:S(2)}, u32[]{:S(2)}) collective-permute-start(f32[4,16,128,128]{3,1,2,0:T(8,128)} %copy.70), channel_id=1, source_target_pairs={{0,8},{8,16},{16,24},{24,32},{32,40},{40,48},{48,56},{56,64},{64,7... | collective-permute-start | bytes 12582920 | tf_op jit(solution)/shard_map/ppermute | solution.py:17
  415.3 50.1 %collective-permute-start.5 = (f32[4,16,128,128]{3,1,2,0:T(8,128)}, f32[4,16,128,128]{3,1,2,0:T(8,128)}, u32[]{:S(2)}, u32[]{:S(2)}) collective-permute-start(f32[4,16,128,128]{3,1,2,0:T(8,128)} %copy.70), channel_id=1, source_target_pairs={{8,0},{16,8},{24,16},{32,24},{40,32},{48,40},{56,48},{64,56},{72,6... | collective-permute-start | bytes 12582920 | tf_op jit(solution)/shard_map/ppermute | solution.py:18
  479.8 38.0 %copy-start.1 = (f32[4,2,128,128]{3,2,0,1:T(8,128)S(1)}, f32[4,2,128,128]{3,2,0,1:T(8,128)}, u32[]{:S(2)}) copy-start(f32[4,2,128,128]{3,2,0,1:T(8,128)} %subtract_select_fusion.2) | copy-start | bytes 1572868
  479.8 38.0 %copy-start.2 = (f32[4,2,128,128]{3,2,0,1:T(8,128)S(1)}, f32[4,2,128,128]{3,2,0,1:T(8,128)}, u32[]{:S(2)}) copy-start(f32[4,2,128,128]{3,2,0,1:T(8,128)} %subtract_select_fusion.1) | copy-start | bytes 1572868
Sparse Core Ops, SparseCore 0:
  10.4 58.6 all-gather.3
  182.9 54.3 all-gather.5
  350.7 54.3 all-gather.7
where the time goes:
time: 608 us; the launch traced here: 606 us
  waiting for transfers between devices  308 us (51%)
  local copies, waits for them, and re-layouts  92 us (15%)
  blocking collectives  77.4 us (13%)
  matrix products  54.5 us (9%)
  loops' own time  31.2 us (5%)
  starting transfers between devices  19.3 us (3%)
  between operations  15.9 us (3%)
  other arithmetic  7.73 us (1%)
    all_gather x3, waiting for transfers between devices, shards(): whole_rows = lax.all_gather(current, 'layer', axis=1, tiled=True)  169 us
    ppermute x3, waiting for transfers between devices, with_halo(): before = lax.ppermute(last, axis, up)  126 us
    psum x1, blocking collectives, shards(): local_traces.append(lax.psum(diag_trace, ('row', 'col', 'layer')))  77.4 us
    gather x12, local copies, waits for them, and re-layouts, one_row(): partner = band[local[:, None], jnp.clip(moved + NEAR, 0, 2 * NEAR)]  43.8 us
    another operation x3, loops' own time, pair_products(): return lax.map(one_row, jnp.arange(own_cols.shape[0], dtype=jnp.int32))  31.2 us
    dot_general x3, matrix products, band_of(): jnp.einsum('hds,hsab->hdab', onehot, rows, precision=lax.Precision.HIGHEST)  27.8 us
    dot_general x12, matrix products, one_row(): jnp.einsum('dac,qdbc->qab', own, partner, precision=lax.Precision.HIGHEST)  26.7 us
    all_gather x3, local copies, waits for them, and re-layouts, shards(): whole_rows = lax.all_gather(current, 'layer', axis=1, tiled=True)  19.7 us
  transfers between devices with their start and end apart: 9, of which 9 were waited for; matrix products, arithmetic and copies ran while one was open for 0% of the time, Pallas kernels for 0%

commit v1 on v0

v1 whole, which is shorter than its diff:
```python
import jax
import jax.numpy as jnp
from jax import lax
from jax.experimental import pallas as pl
from jax.experimental.pallas import tpu as pltpu
from jax.sharding import PartitionSpec as P

MESH = pl.DeviceIdType.MESH
B = 128
H = 4
D = 5
STEPS = 3
LEFT_TILES = ((0, 0, (4, 10), (0, 4)), (0, 1, (4, 10), (2, 4)), (1, 1, (4, 12), (2, 4)))
RIGHT_TILES = ((0, 2, (4, 8), (8, 10)), (1, 2, (4, 8), (8, 12)), (1, 3, (6, 8), (8, 12)))
TILES = LEFT_TILES + RIGHT_TILES
UPPER = tuple((a, d) for a in range(H) for d in range(D))
INNER = tuple((a, d) for a, d in UPPER if a + d < H)
OUTER = tuple((a, d) for a, d in UPPER if a + d >= H)


def at_layer(group):
    return 4 * lax.rem(group // 2 + group, 2)


def kernel(groups, n_col, n_layer, cols_ref, signs_ref, blk_ref, out_ref, tr_ref, own, left, right, high, low, acc, flip,
           zero, tb1, tb2, tb3, gsend, grecv, hsend, hrecv, osend, orecv, zsem, t1s, t1r, t2s, t2r, t3s, t3r):
    row, col, layer = lax.axis_index("row"), lax.axis_index("col"), lax.axis_index("layer")
    n_row = groups // n_col
    g = row * n_col + col
    after, before = lax.rem(g + 1, groups), lax.rem(g + groups - 1, groups)
    zc = at_layer(g)
    collector = layer == zc
    base = lax.rem(H * g, n_layer)
    u = lax.rem(layer - base + n_layer, n_layer)

    def place(group, at):
        return (group // n_col, lax.rem(group, n_col), at)

    def head(group):
        return place(group, at_layer(group))

    def slot_up(group):
        return jnp.where(group == 0, 0, 1)

    def remote(src, dst, send, recv, to):
        return pltpu.make_async_remote_copy(src, dst, send, recv, device_id=to, device_id_type=MESH)

    def arrived(ref, sem):
        pltpu.make_async_copy(ref, ref, sem).wait()

    barrier = pltpu.get_barrier_semaphore()

    def greet(to):
        pl.semaphore_signal(barrier, inc=1, device_id=to, device_id_type=MESH)

    greet(head(before))

    @pl.when(jnp.logical_not(collector))
    def _():
        greet(head(g))
        pl.semaphore_wait(barrier, 1)

    @pl.when(collector)
    def _():
        greet(head(after))
        for p in range(1, n_layer):
            greet(place(g, lax.rem(layer + p, n_layer)))
        for p in range(1, n_col):
            greet(head(row * n_col + lax.rem(col + p, n_col)))
        for p in range(1, n_row):
            greet(head(lax.rem(row + p, n_row) * n_col + col))
        pl.semaphore_wait(barrier, (n_layer - 1) + n_layer + 1 + (n_col - 1) + (n_row - 1))

    def source(a):
        d = u - a
        return d, jnp.where(d == D - 1, slot_up(g), 0)

    for a in range(H):
        d, slot = source(a)
        has = (d >= 0) & (d < D)

        @pl.when(has & jnp.logical_not(collector))
        def _():
            remote(blk_ref.at[a, slot], own.at[0, a, d], gsend.at[a], grecv.at[a, d], head(g)).start()

        @pl.when(has & collector)
        def _():
            pltpu.make_async_copy(blk_ref.at[a, slot], own.at[0, a, d], grecv.at[a, d]).start()

    zero[...] = jnp.zeros_like(zero)
    for a in range(H):
        @pl.when(u != a + H)
        def _():
            pltpu.make_async_copy(zero, out_ref.at[a, 1], zsem.at[a]).start()

    def to_before(t, a):
        part = pl.ds(0, H - a)
        return remote(own.at[t, a, part], right.at[t, a, part], hsend.at[t, 0, a], hrecv.at[t, 0, a], head(before))

    def to_after(t, a):
        part = pl.ds(H - a, a + 1)
        return remote(own.at[t, a, part], left.at[t, a, part], hsend.at[t, 1, a], hrecv.at[t, 1, a], head(after))

    def put(r, k, x):
        h = x.astype(jnp.bfloat16)
        high[r * B:(r + 1) * B, k * B:(k + 1) * B] = h
        low[r * B:(r + 1) * B, k * B:(k + 1) * B] = (x - h.astype(jnp.float32)).astype(jnp.bfloat16)

    def product(i, j, span):
        def part(ref, r):
            return ref[2 * B * r:2 * B * (r + 1), span[0] * B:span[1] * B]

        def dot(x, y):
            return lax.dot_general(x, y, (((1,), (1,)), ((), ())), preferred_element_type=jnp.float32)

        ah, al, bh, bl = part(high, i), part(low, i), part(high, j), part(low, j)
        return dot(ah, bh) + (dot(al, bh) + dot(ah, bl))

    def finish(t, tiles):
        square = signs_ref[t] == 1
        keep = jnp.where(square, 0.0, 2.0).astype(jnp.float32)
        sign = jnp.where(square, 1.0, -1.0).astype(jnp.float32)
        for i, j, inner, outer in tiles:
            n = TILES.index((i, j, inner, outer))
            tile = acc[n] + product(i, j, outer)
            for a in (2 * i, 2 * i + 1):
                for q in (2 * j, 2 * j + 1):
                    d = q - a
                    if 0 <= d < D:
                        at_row = H * g + a
                        at_col = at_row + d
                        slot = 2 * lax.rem(at_col, n_layer)
                        there = (cols_ref[at_row, slot] == at_col) | (cols_ref[at_row, slot + 1] == at_col)
                        factor = jnp.where(there, sign, 0.0)
                        part = tile[(a % 2) * B:(a % 2 + 1) * B, (q % 2) * B:(q % 2 + 1) * B]
                        own[t + 1, a, d] = keep * own[t, a, d] + factor * part

    def share_traces():
        eye = lax.broadcasted_iota(jnp.int32, (B, B), 0) == lax.broadcasted_iota(jnp.int32, (B, B), 1)

        def diagonal(t):
            total = own[t, 0, 0]
            for a in range(1, H):
                total = total + own[t, a, 0]
            return jnp.sum(jnp.where(eye, total, 0.0), axis=0, keepdims=True)

        one, two = diagonal(1), diagonal(2)
        diag = jnp.zeros((B, B), jnp.float32)
        off = jnp.zeros((B, B), jnp.float32)
        for a, d in UPPER:
            x = own[2, a, d]
            if d:
                off = off + x * x
            else:
                diag = diag + x * x
        norm = jnp.sum(diag + 2.0 * off, axis=0, keepdims=True)
        three = jnp.where(signs_ref[2] == 1, norm, 2.0 * two - norm)
        line = lax.broadcasted_iota(jnp.int32, (8, B), 0)
        tb1[col] = jnp.where(line == 0, one, jnp.where(line == 1, two, jnp.where(line == 2, three, 0.0)))
        for p in range(1, n_col):
            to = head(row * n_col + lax.rem(col + p, n_col))
            remote(tb1.at[col], tb1.at[col], t1s.at[p], t1r.at[col], to).start()

    def share_rows():
        for p in range(1, n_col):
            c = lax.rem(col + p, n_col)
            arrived(tb1.at[c], t1r.at[c])
        tb2[row] = jnp.sum(tb1[...], axis=0)
        for p in range(1, n_row):
            to = head(lax.rem(row + p, n_row) * n_col + col)
            remote(tb2.at[row], tb2.at[row], t2s.at[p], t2r.at[row], to).start()

    def share_layers():
        for p in range(1, n_row):
            r = lax.rem(row + p, n_row)
            arrived(tb2.at[r], t2r.at[r])
        total = jnp.sum(jnp.sum(tb2[...], axis=0), axis=1, keepdims=True) / (groups * H * B)
        tb3[...] = jnp.broadcast_to(total, (8, B))
        for p in range(1, n_layer):
            remote(tb3, tb3, t3s.at[p], t3r, place(g, lax.rem(layer + p, n_layer))).start()

    @pl.when(collector)
    def _():
        high[...] = jnp.zeros_like(high)
        low[...] = jnp.zeros_like(low)
        for a in range(H):
            for d in range(H - a):
                arrived(own.at[0, a, d], grecv.at[a, d])
            to_before(0, a).start()
        for a in range(H):
            for d in range(H - a, D):
                arrived(own.at[0, a, d], grecv.at[a, d])
            to_after(0, a).start()

        def step(t, carry):
            for a, d in UPPER:
                x = own[t, a, d]
                put(a, H + a + d, x)
                if d:
                    put(a + d, H + a, x.T)
            pl.when(t == 2)(share_traces)
            for n, (i, j, inner, _) in enumerate(TILES):
                acc[n] = product(i, j, inner)
            pl.when(t == 2)(share_rows)
            for a in range(H):
                part = pl.ds(H - a, a + 1)
                arrived(left.at[t, a, part], hrecv.at[t, 1, a])
            for a, d in OUTER:
                put(a + d - H, a, left[t, a, d].T)
            finish(t, LEFT_TILES)

            @pl.when(t < 2)
            def _():
                for a in range(H):
                    to_before(t + 1, a).start()

            for a in range(H):
                part = pl.ds(0, H - a)
                arrived(right.at[t, a, part], hrecv.at[t, 0, a])
            for a, d in INNER:
                x = right[t, a, d]
                put(H + a, 2 * H + a + d, x)
                if d:
                    put(H + a + d, 2 * H + a, x.T)
            finish(t, RIGHT_TILES)

            @pl.when(t < 2)
            def _():
                for a in range(H):
                    to_after(t + 1, a).start()

            pl.when(t == 2)(share_layers)
            return carry

        lax.fori_loop(0, STEPS, step, 0)

        for a, d in UPPER:
            if d:
                flip[a, d] = own[STEPS, a, d].T

        for done in (False, True):
            for a, d in UPPER:
                q = a + d
                way = [(0, own.at[STEPS, a, d], g, lax.rem(base + q, n_layer), a, slot_up(g) if d == H else 0)]
                if d:
                    src = flip.at[a, d]
                    if q < H:
                        way.append((1, src, g, lax.rem(base + a, n_layer), q, 0))
                    else:
                        slot = 1 - slot_up(after) if d == H else 0
                        way.append((1, src, after, lax.rem(base + a, n_layer), q - H, slot))
                for n, src, group, at, r, slot in way:
                    sem = osend.at[n, a, d]
                    far = remote(src, out_ref.at[r, slot], sem, orecv.at[r, slot], place(group, at))
                    if n == 1 and q >= H:
                        far.wait_send() if done else far.start()
                        continue
                    here = at == layer

                    @pl.when(jnp.logical_not(here))
                    def _():
                        far.wait_send() if done else far.start()

                    if not done:
                        @pl.when(here)
                        def _():
                            pltpu.make_async_copy(src, out_ref.at[r, slot], orecv.at[r, slot]).start()

        for t in range(STEPS):
            for a in range(H):
                to_before(t, a).wait_send()
                to_after(t, a).wait_send()
        for p in range(1, n_col):
            remote(tb1.at[col], tb1.at[col], t1s.at[p], t1r.at[col], head(g)).wait_send()
        for p in range(1, n_row):
            remote(tb2.at[row], tb2.at[row], t2s.at[p], t2r.at[row], head(g)).wait_send()
        for p in range(1, n_layer):
            remote(tb3, tb3, t3s.at[p], t3r, head(g)).wait_send()

    @pl.when(jnp.logical_not(collector))
    def _():
        for a in range(H):
            d, slot = source(a)

            @pl.when((d >= 0) & (d < D))
            def _():
                remote(blk_ref.at[a, slot], own.at[0, a, d], gsend.at[a], grecv.at[a, d], head(g)).wait_send()

        arrived(tb3, t3r)

    for t in range(STEPS):
        tr_ref[t] = tb3[t, 0]
    for a in range(H):
        arrived(out_ref.at[a, 0], orecv.at[a, 0])

        @pl.when(u == a + H)
        def _():
            arrived(out_ref.at[a, 1], orecv.at[a, 1])

        @pl.when(u != a + H)
        def _():
            pltpu.make_async_copy(zero, out_ref.at[a, 1], zsem.at[a]).wait()


def solution(mesh):
    n_row, n_col, n_layer = (mesh.shape[name] for name in ("row", "col", "layer"))
    groups = n_row * n_col
    dma = pltpu.SemaphoreType.DMA

    def shards(blocks, columns, signs):
        def body(*refs):
            kernel(groups, n_col, n_layer, *refs)

        f32, bf16 = jnp.float32, jnp.bfloat16
        return pl.pallas_call(
            body,
            out_shape=(jax.ShapeDtypeStruct(blocks.shape, f32), jax.ShapeDtypeStruct((STEPS,), f32)),
            in_specs=[
                pl.BlockSpec(memory_space=pltpu.SMEM),
                pl.BlockSpec(memory_space=pltpu.SMEM),
                pl.BlockSpec(memory_space=pl.ANY),
            ],
            out_specs=(pl.BlockSpec(memory_space=pl.ANY), pl.BlockSpec(memory_space=pltpu.SMEM)),
            scratch_shapes=[
                pltpu.VMEM((STEPS + 1, H, D, B, B), f32),
                pltpu.VMEM((STEPS, H, D, B, B), f32),
                pltpu.VMEM((STEPS, H, D, B, B), f32),
                pltpu.VMEM((2 * H * B, 3 * H * B), bf16),
                pltpu.VMEM((2 * H * B, 3 * H * B), bf16),
                pltpu.VMEM((len(TILES), 2 * B, 2 * B), f32),
                pltpu.VMEM((H, D, B, B), f32),
                pltpu.VMEM((B, B), f32),
                pltpu.VMEM((n_col, 8, B), f32),
                pltpu.VMEM((n_row, 8, B), f32),
                pltpu.VMEM((8, B), f32),
                dma((H,)),
                dma((H, D)),
                dma((STEPS, 2, H)),
                dma((STEPS, 2, H)),
                dma((2, H, D)),
                dma((H, 2)),
                dma((H,)),
                dma((n_col,)),
                dma((n_col,)),
                dma((n_row,)),
                dma((n_row,)),
                dma((n_layer,)),
                dma,
            ],
            compiler_params=pltpu.CompilerParams(
                collective_id=0, has_side_effects=True, vmem_limit_bytes=48 * 1024 * 1024
            ),
        )(columns, signs, blocks)

    return jax.shard_map(
        shards,
        mesh=mesh,
        in_specs=(P(("row", "col"), "layer", None, None), P(), P()),
        out_specs=(P(("row", "col"), "layer", None, None), P()),
        check_vma=False,
    )
```

time: 608 us -> 92.3 us (0.15)
  waiting for transfers between devices: 308 us -> 0 us
  local copies, waits for them, and re-layouts: 92 us -> 3.15 us
  Pallas kernels: 0 us -> 88.2 us
  blocking collectives: 77.4 us -> 0 us
  matrix products: 54.5 us -> 0 us
  loops' own time: 31.2 us -> 0 us
  starting transfers between devices: 19.3 us -> 0 us
  between operations: 15.9 us -> 0.66 us
  other arithmetic: 7.73 us -> 0 us
    all_gather x3 -> x0, waiting for transfers between devices: 169 us -> none  [shards(): whole_rows = lax.all_gather(current, 'layer', axis=1, tiled=True)]
    ppermute x6 -> x0, waiting for transfers between devices: 139 us -> none  [the longest x3 126 us: with_halo(): before = lax.ppermute(last, axis, up)]
    pallas_call x0 -> x1, Pallas kernels: none -> 88.2 us  [shards(): pl.pallas_call(body, out_shape=(jax.ShapeDtypeStruct(blocks.shape, f32),...]
    psum x1 -> x0, blocking collectives: 77.4 us -> none  [shards(): local_traces.append(lax.psum(diag_trace, ('row', 'col', 'layer')))]
    dot_general x15 -> x0, matrix products: 54.5 us -> none  [the longest x3 27.8 us: band_of(): jnp.einsum('hds,hsab->hdab', onehot, rows, precision=lax.Precision.HIGHEST)]
    gather x12 -> x0, local copies, waits for them, and re-layouts: 43.8 us -> none  [one_row(): partner = band[local[:, None], jnp.clip(moved + NEAR, 0, 2 * NEAR)]]
    another operation x3 -> x0, loops' own time: 31.2 us -> none  [pair_products(): return lax.map(one_row, jnp.arange(own_cols.shape[0], dtype=jnp.int32))]
    all_gather x3 -> x0, local copies, waits for them, and re-layouts: 19.7 us -> none  [shards(): whole_rows = lax.all_gather(current, 'layer', axis=1, tiled=True)]
  transfers between devices with their start and end apart: 9 -> 0, of which waited for: 9 -> 0; matrix products, arithmetic and copies ran while one was open for 0% -> 0% of each run, Pallas kernels for 0% -> 0%
where the time goes in v1:
time: 92.3 us; the launch traced here: 92 us
  Pallas kernels  88.2 us (96%)
  local copies, waits for them, and re-layouts  3.15 us (3%)
    pallas_call x1, Pallas kernels, shards(): pl.pallas_call(body, out_shape=(jax.ShapeDtypeStruct(blocks.shape, f32),...  88.2 us
    unnamed x7, local copies, waits for them, and re-layouts  3.15 us

profile of v1, /device:TPU:1, one launch (start us, length us, event | category | flops | bytes accessed | tf_op | source)
XLA Modules:
  0.0 92.0 jit_solution(13756580760799296893)
XLA Ops:
  0.6 0.0 copy-start.1
  0.6 0.8 copy.5.refs_0_
  1.4 0.0 copy-done.1
  1.4 0.0 copy-start
  1.5 1.0 %copy-done = f32[4,2,128,128]{3,2,1,0:T(8,128)S(1)} copy-done((f32[4,2,128,128]{3,2,1,0:T(8,128)S(1)}, f32[4,2,128,128]{3,2,1,0:T(8,128)}, u32[]{:S(2)}) %copy-start) | copy-done | bytes 524312
  2.5 88.2 %shard_map.50 = (f32[4,2,128,128]{3,2,1,0:T(8,128)S(1)}, f32[3]{0:T(128)S(1)}) custom-call(s32[128,16]{1,0:T(8,128)S(1)} %copy.5.refs_0_, s32[3]{0:T(128)S(1)} %copy-done.1, f32[4,2,128,128]{3,2,1,0:T(8,128)S(1)} %copy-done), custom_call_target="tpu_custom_call" | custom-call | tf_op jit(solution)/shard_map/pallas_call | solution.py:315
  90.7 0.8 copy.8
  91.5 0.5 copy.9
Async XLA Ops:
  0.6 0.8 copy-start.1
  1.4 1.0 %copy-start = (f32[4,2,128,128]{3,2,1,0:T(8,128)S(1)}, f32[4,2,128,128]{3,2,1,0:T(8,128)}, u32[]{:S(2)}) copy-start(f32[4,2,128,128]{3,2,1,0:T(8,128)} %refs_2_.1) | copy-start | bytes 1572868

commit v2 on v0

v2 whole, which is shorter than its diff:
```python
import jax
import jax.numpy as jnp
from jax import lax
from jax.experimental import pallas as pl
from jax.experimental.pallas import tpu as pltpu
from jax.sharding import PartitionSpec as P

MESH = pl.DeviceIdType.MESH
B = 128
ROWS = 4
STEPS = 3
BLOCKS = ((0, 0), (0, 1), (1, 1), (0, 2), (0, 3), (1, 2), (1, 3), (0, 4), (1, 4), (1, 5))
SPAN = {"A": (0, 3), "B": (3, 4), "C": (7, 3)}
TILE = {"A": 0, "B": 1, "C": 2}
COPIES = (("B", -1), ("B", 1), ("A", -1), ("C", 1), ("A", -2), ("C", 2))


def kernel(n_row, n_col, n_layer, cols_ref, signs_ref, blk_ref, out_ref, tr_ref, own, left1, left2, right1, right2, high, low,
           acc, flip, zero, mine, tb0, tb1, tb2, tb3, gsend, grecv, hsend, hrecv, osend, orecv, zsem, t0s, t0r, t1s, t1r, t2s, t2r,
           t3s, t3r):
    row, col, layer = lax.axis_index("row"), lax.axis_index("col"), lax.axis_index("layer")
    i32 = jnp.int32
    core = lax.rem(col, 2)
    base = 4 * core
    u = jnp.where(layer < base, layer - base + n_layer, layer - base)
    collector = (u == 1) | (u == 3)
    b = jnp.where(u == 3, 1, 0)
    first = (row == 0) & (col == 0)
    last = (row == n_row - 1) & (col == n_col - 1)
    wrap_up, wrap_down = col == n_col - 1, col == 0
    up = (jnp.where(wrap_up, jnp.where(row == n_row - 1, 0, row + 1), row), jnp.where(wrap_up, 0, col + 1))
    down = (jnp.where(wrap_down, jnp.where(row == 0, n_row - 1, row - 1), row), jnp.where(wrap_down, n_col - 1, col - 1))
    here = (row, col)
    far = 4 - base

    def pick(cond, x, y):
        return tuple(jnp.where(cond, p, q) for p, q in zip(x, y))

    peer = {
        1: pick(b == 0, (*here, base + 3), (*up, far + 1)),
        2: (*up, far + 1 + 2 * b),
        -1: pick(b == 0, (*down, far + 3), (*here, base + 1)),
        -2: (*down, far + 1 + 2 * b),
    }
    slot_up = jnp.where(first, 0, 1)
    slot_down = jnp.where(last, 1, 0)

    def turn(x, p, n):
        return jnp.where(x + p >= n, x + p - n, x + p)

    def remote(src, dst, send, recv, to):
        return pltpu.make_async_remote_copy(src, dst, send, recv, device_id=to, device_id_type=MESH)

    def arrived(ref, sem):
        pltpu.make_async_copy(ref, ref, sem).wait()

    others = [(row, col, turn(layer, p, n_layer)) for p in range(1, n_layer)]
    col_peers = [(row, turn(col, p, n_col), jnp.where(lax.rem(col + p, 2) == 0, 1, 5)) for p in range(1, n_col)]
    row_peers = [(turn(row, p, n_row), col, base + 1) for p in range(1, n_row)]

    barrier = pltpu.get_barrier_semaphore()

    def greet(to):
        pl.semaphore_signal(barrier, inc=1, device_id=to, device_id_type=MESH)

    @pl.when(collector)
    def _():
        for to in others:
            greet(to)

    for k in range(2):
        @pl.when(u != 1 + 2 * k)
        def _():
            greet((*here, base + 1 + 2 * k))

        greet((*down, far + 1 + 2 * k))

    @pl.when(collector)
    def _():
        for to in peer.values():
            greet(to)
        want = 1 + (n_layer - 1) + n_layer + 4

        @pl.when(b == 0)
        def _():
            for to in col_peers + row_peers:
                greet(to)
            pl.semaphore_wait(barrier, want + (n_col - 1) + (n_row - 1))

        @pl.when(b == 1)
        def _():
            pl.semaphore_wait(barrier, want)

    @pl.when(jnp.logical_not(collector))
    def _():
        pl.semaphore_wait(barrier, 2)

    def source(a):
        d = u - a
        q = u - 2 * (a // 2)
        two, four = jnp.where(q >= 2, 1, 0), jnp.where(q >= 4, 1, 0)
        n = q + 1 + 2 * two + four if a % 2 else q + two + 2 * four
        slot = jnp.where(d == ROWS, slot_up, 0)
        has = (d >= 0) & (d <= ROWS)
        return has, blk_ref.at[a, slot], n, (*here, base + 1 + 2 * (a // 2)), u == 1 + 2 * (a // 2)

    for a in range(ROWS):
        has, block, n, to, local = source(a)

        @pl.when(has & jnp.logical_not(local))
        def _():
            remote(block, own.at[0, n], gsend.at[a], grecv.at[n], to).start()

        @pl.when(has & local)
        def _():
            pltpu.make_async_copy(block, own.at[0, n], grecv.at[n]).start()

    zero[...] = jnp.zeros_like(zero)
    for a in range(ROWS):
        @pl.when(u != a + ROWS)
        def _():
            pltpu.make_async_copy(zero, out_ref.at[a, 1], zsem.at[a]).start()

    def landing(k, t):
        tile, to = COPIES[k]
        if to == 2:
            return left2.at[t]
        if to == -2:
            return right2.at[t]
        start, size = SPAN[tile]
        return left1.at[t, pl.ds(start - 3, size)] if to == 1 else right1.at[t, pl.ds(start, size)]

    def copy(k, t):
        tile, to = COPIES[k]
        start, size = SPAN[tile]
        return remote(own.at[t, pl.ds(start, size)], landing(k, t), hsend.at[t, k], hrecv.at[t, k], peer[to])

    def await_halo(k, t):
        arrived(landing(k, t), hrecv.at[t, k])

    def put(r, k, x):
        h = x.astype(jnp.bfloat16)
        lo = (x - h.astype(jnp.float32)).astype(jnp.bfloat16)
        high[r * B:(r + 1) * B, (k + 4) * B:(k + 5) * B] = h
        low[r * B:(r + 1) * B, (k + 4) * B:(k + 5) * B] = lo

    def put_both(r, k, x):
        put(r, k, x)
        if k > r:
            put(k, r, x.T)

    def product(tile, start, stop):
        j = 2 * TILE[tile]

        def part(ref, r):
            return ref[r * B:(r + 2) * B, (start + 4) * B:(stop + 4) * B]

        def dot(x, y):
            return lax.dot_general(x, y, (((1,), (1,)), ((), ())), preferred_element_type=jnp.float32)

        ah, al, bh, bl = part(high, 0), part(low, 0), part(high, j), part(low, j)
        return dot(ah, bh) + (dot(al, bh) + dot(ah, bl))

    def there(a, q):
        at_row = ROWS * (row * n_col + col) + 2 * b + a
        at_col = at_row + q - a
        slot = 2 * turn(base + 2 * b, q, n_layer)
        return (cols_ref[slot, at_row] == at_col) | (cols_ref[slot + 1, at_row] == at_col)

    def finish(t, tile, total):
        square = signs_ref[t] == 1
        keep = jnp.where(square, 0.0, 2.0).astype(jnp.float32)
        sign = jnp.where(square, 1.0, -1.0).astype(jnp.float32)
        start, size = SPAN[tile]
        for n in range(start, start + size):
            a, q = BLOCKS[n]
            factor = jnp.where(there(a, q), sign, 0.0)
            part = total[a * B:(a + 1) * B, (q % 2) * B:(q % 2 + 1) * B]
            own[t + 1, n] = keep * own[t, n] + factor * part

    def results(tile):
        start, size = SPAN[tile]
        for n in range(start, start + size):
            a, q = BLOCKS[n]
            slot = slot_up if q - a == ROWS else 0
            dst = out_ref.at[2 * b + a, slot]
            sem = orecv.at[2 * b + a, slot]
            src = own.at[STEPS, n]
            yield src, dst, osend.at[0, n], sem, (*here, turn(base + 2 * b, q, n_layer)), q == 1
            if q > a:
                over = 2 * b + q >= ROWS
                r = jnp.where(over, 2 * b + q - ROWS, 2 * b + q)
                slot = slot_down if q - a == ROWS else 0
                to = pick(over, up, here)
                local = (b == 0) if a == 1 and q < ROWS else False
                yield flip.at[n], out_ref.at[r, slot], osend.at[1, n], orecv.at[r, slot], (*to, base + 2 * b + a), local

    def deliver(tile):
        start, size = SPAN[tile]
        for n in range(start, start + size):
            a, q = BLOCKS[n]
            if q > a:
                flip[n] = own[STEPS, n].T
        for src, dst, send, recv, to, local in results(tile):
            if local is not True:
                @pl.when(jnp.logical_not(local))
                def _():
                    remote(src, dst, send, recv, to).start()
            if local is not False:
                @pl.when(local)
                def _():
                    pltpu.make_async_copy(src, dst, recv).start()

    def delivered(tile):
        for src, dst, send, recv, to, local in results(tile):
            if local is not True:
                @pl.when(jnp.logical_not(local))
                def _():
                    remote(src, dst, send, recv, to).wait_send()

    def share_pair():
        eye = lax.broadcasted_iota(i32, (B, B), 0) == lax.broadcasted_iota(i32, (B, B), 1)

        def diagonal(t):
            return jnp.sum(jnp.where(eye, own[t, 0] + own[t, 2], 0.0), axis=0, keepdims=True)

        one, two = diagonal(1), diagonal(2)
        diag = jnp.zeros((B, B), jnp.float32)
        off = jnp.zeros((B, B), jnp.float32)
        for n, (a, q) in enumerate(BLOCKS):
            x = own[2, n]
            if q > a:
                off = off + x * x
            else:
                diag = diag + x * x
        norm = jnp.sum(diag + 2.0 * off, axis=0, keepdims=True)
        three = jnp.where(signs_ref[2] == 1, norm, 2.0 * two - norm)
        line = lax.broadcasted_iota(i32, (8, B), 0)
        mine[...] = jnp.where(line == 0, one, jnp.where(line == 1, two, jnp.where(line == 2, three, 0.0)))

        @pl.when(b == 1)
        def _():
            remote(mine, tb0, t0s, t0r, (*here, base + 1)).start()

    def share_cols():
        arrived(tb0, t0r)
        tb1[col] = mine[...] + tb0[...]
        for p, to in enumerate(col_peers):
            remote(tb1.at[col], tb1.at[col], t1s.at[p], t1r.at[col], to).start()

    def share_rows():
        for p in range(1, n_col):
            c = turn(col, p, n_col)
            arrived(tb1.at[c], t1r.at[c])
        tb2[row] = jnp.sum(tb1[...], axis=0)
        for p, to in enumerate(row_peers):
            remote(tb2.at[row], tb2.at[row], t2s.at[p], t2r.at[row], to).start()

    def share_layers():
        for p in range(1, n_row):
            r = turn(row, p, n_row)
            arrived(tb2.at[r], t2r.at[r])
        total = jnp.sum(jnp.sum(tb2[...], axis=0), axis=1, keepdims=True) / (n_row * n_col * ROWS * B)
        mine[...] = jnp.broadcast_to(total, (8, B))
        for p, to in enumerate(others):
            remote(mine, tb3, t3s.at[p], t3r, to).start()

    @pl.when(collector)
    def _():
        for r, k in ((0, 5), (1, -4), (3, -2), (5, 0)):
            put(r, k, jnp.zeros((B, B), jnp.float32))
        for tile, ks in (("B", (0, 1)), ("A", (2, 4)), ("C", (3, 5))):
            start, size = SPAN[tile]
            for n in range(start, start + size):
                arrived(own.at[0, n], grecv.at[n])
            for k in ks:
                copy(k, 0).start()

        def step(t, carry):
            for n, (a, q) in enumerate(BLOCKS):
                put_both(a, q, own[t, n])
            pl.when(t == 2)(share_pair)
            acc[0] = product("A", 0, 6)
            acc[1] = product("B", 0, 2)
            acc[2] = product("C", 0, 2)
            pl.when((t == 2) & (b == 0))(share_cols)

            def after(tile, ks):
                @pl.when(t < 2)
                def _():
                    for k in ks:
                        copy(k, t + 1).start()

                @pl.when(t == 2)
                def _():
                    deliver(tile)

            await_halo(1, t)
            await_halo(3, t)
            for n in range(3, 10):
                a, q = BLOCKS[n]
                put(q - 2, a - 2, left1[t, n - 3].T)
            await_halo(0, t)
            await_halo(2, t)
            for n in range(7):
                a, q = BLOCKS[n]
                put_both(a + 2, q + 2, right1[t, n])
            finish(t, "B", acc[1] + product("B", -2, 0) + product("B", 2, 6))
            after("B", (0, 1))
            await_halo(5, t)
            for n in range(7, 10):
                a, q = BLOCKS[n]
                put(q - 4, a - 4, left2[t, n - 7].T)
            finish(t, "A", acc[0] + product("A", -4, 0))
            after("A", (2, 4))
            await_halo(4, t)
            for n in range(3):
                a, q = BLOCKS[n]
                put_both(a + 4, q + 4, right2[t, n])
            finish(t, "C", acc[2] + product("C", 2, 6))
            after("C", (3, 5))
            return carry

        lax.fori_loop(0, STEPS, step, 0)

        @pl.when(b == 0)
        def _():
            share_rows()
            share_layers()

        for t in range(STEPS):
            for k in range(len(COPIES)):
                copy(k, t).wait_send()
        for tile in SPAN:
            delivered(tile)

        @pl.when(b == 0)
        def _():
            for p, to in enumerate(col_peers):
                remote(tb1.at[col], tb1.at[col], t1s.at[p], t1r.at[col], to).wait_send()
            for p, to in enumerate(row_peers):
                remote(tb2.at[row], tb2.at[row], t2s.at[p], t2r.at[row], to).wait_send()
            for p, to in enumerate(others):
                remote(mine, tb3, t3s.at[p], t3r, to).wait_send()
            tb3[...] = mine[...]

        @pl.when(b == 1)
        def _():
            remote(mine, tb0, t0s, t0r, (*here, base + 1)).wait_send()

    for a in range(ROWS):
        has, block, n, to, local = source(a)

        @pl.when(has & jnp.logical_not(local))
        def _():
            remote(block, own.at[0, n], gsend.at[a], grecv.at[n], to).wait_send()

    @pl.when(u != 1)
    def _():
        arrived(tb3, t3r)

    for t in range(STEPS):
        tr_ref[t] = tb3[t, 0]
    for a in range(ROWS):
        arrived(out_ref.at[a, 0], orecv.at[a, 0])

        @pl.when(u == a + ROWS)
        def _():
            arrived(out_ref.at[a, 1], orecv.at[a, 1])

        @pl.when(u != a + ROWS)
        def _():
            pltpu.make_async_copy(zero, out_ref.at[a, 1], zsem.at[a]).wait()


def solution(mesh):
    n_row, n_col, n_layer = (mesh.shape[name] for name in ("row", "col", "layer"))
    dma = pltpu.SemaphoreType.DMA

    def shards(blocks, columns, signs):
        def body(*refs):
            kernel(n_row, n_col, n_layer, *refs)

        f32, bf16 = jnp.float32, jnp.bfloat16
        return pl.pallas_call(
            body,
            out_shape=(jax.ShapeDtypeStruct(blocks.shape, f32), jax.ShapeDtypeStruct((STEPS,), f32)),
            in_specs=[
                pl.BlockSpec(memory_space=pltpu.SMEM),
                pl.BlockSpec(memory_space=pltpu.SMEM),
                pl.BlockSpec(memory_space=pl.ANY),
            ],
            out_specs=(pl.BlockSpec(memory_space=pl.ANY), pl.BlockSpec(memory_space=pltpu.SMEM)),
            scratch_shapes=[
                pltpu.VMEM((STEPS + 1, 10, B, B), f32),
                pltpu.VMEM((STEPS, 7, B, B), f32),
                pltpu.VMEM((STEPS, 3, B, B), f32),
                pltpu.VMEM((STEPS, 7, B, B), f32),
                pltpu.VMEM((STEPS, 3, B, B), f32),
                pltpu.VMEM((6 * B, 10 * B), bf16),
                pltpu.VMEM((6 * B, 10 * B), bf16),
                pltpu.VMEM((3, 2 * B, 2 * B), f32),
                pltpu.VMEM((10, B, B), f32),
                pltpu.VMEM((B, B), f32),
                pltpu.VMEM((8, B), f32),
                pltpu.VMEM((8, B), f32),
                pltpu.VMEM((n_col, 8, B), f32),
                pltpu.VMEM((n_row, 8, B), f32),
                pltpu.VMEM((8, B), f32),
                dma((ROWS,)),
                dma((10,)),
                dma((STEPS, len(COPIES))),
                dma((STEPS, len(COPIES))),
                dma((2, 10)),
                dma((ROWS, 2)),
                dma((ROWS,)),
                dma,
                dma,
                dma((n_col,)),
                dma((n_col,)),
                dma((n_row,)),
                dma((n_row,)),
                dma((n_layer,)),
                dma,
            ],
            compiler_params=pltpu.CompilerParams(
                collective_id=0, has_side_effects=True, vmem_limit_bytes=60 * 1024 * 1024
            ),
        )(columns.T, signs, blocks)

    return jax.shard_map(
        shards,
        mesh=mesh,
        in_specs=(P(("row", "col"), "layer", None, None), P(), P()),
        out_specs=(P(("row", "col"), "layer", None, None), P()),
        check_vma=False,
    )
```

time: 608 us -> 84.1 us (0.14)
  waiting for transfers between devices: 308 us -> 0 us
  local copies, waits for them, and re-layouts: 92 us -> 2.39 us
  Pallas kernels: 0 us -> 80.9 us
  blocking collectives: 77.4 us -> 0 us
  matrix products: 54.5 us -> 0 us
  loops' own time: 31.2 us -> 0 us
  starting transfers between devices: 19.3 us -> 0 us
  between operations: 15.9 us -> 0.65 us
  other arithmetic: 7.73 us -> 0 us
    all_gather x3 -> x0, waiting for transfers between devices: 169 us -> none  [shards(): whole_rows = lax.all_gather(current, 'layer', axis=1, tiled=True)]
    ppermute x6 -> x0, waiting for transfers between devices: 139 us -> none  [the longest x3 126 us: with_halo(): before = lax.ppermute(last, axis, up)]
    pallas_call x0 -> x1, Pallas kernels: none -> 80.9 us  [shards(): pl.pallas_call(body, out_shape=(jax.ShapeDtypeStruct(blocks.shape, f32),...]
    psum x1 -> x0, blocking collectives: 77.4 us -> none  [shards(): local_traces.append(lax.psum(diag_trace, ('row', 'col', 'layer')))]
    dot_general x15 -> x0, matrix products: 54.5 us -> none  [the longest x3 27.8 us: band_of(): jnp.einsum('hds,hsab->hdab', onehot, rows, precision=lax.Precision.HIGHEST)]
    gather x12 -> x0, local copies, waits for them, and re-layouts: 43.8 us -> none  [one_row(): partner = band[local[:, None], jnp.clip(moved + NEAR, 0, 2 * NEAR)]]
    another operation x3 -> x0, loops' own time: 31.2 us -> none  [pair_products(): return lax.map(one_row, jnp.arange(own_cols.shape[0], dtype=jnp.int32))]
    all_gather x3 -> x0, local copies, waits for them, and re-layouts: 19.7 us -> none  [shards(): whole_rows = lax.all_gather(current, 'layer', axis=1, tiled=True)]
  transfers between devices with their start and end apart: 9 -> 0, of which waited for: 9 -> 0; matrix products, arithmetic and copies ran while one was open for 0% -> 0% of each run, Pallas kernels for 0% -> 0%
where the time goes in v2:
time: 84.1 us; the launch traced here: 84 us
  Pallas kernels  80.9 us (96%)
  local copies, waits for them, and re-layouts  2.39 us (3%)
    pallas_call x1, Pallas kernels, shards(): pl.pallas_call(body, out_shape=(jax.ShapeDtypeStruct(blocks.shape, f32),...  80.9 us
    unnamed x4, local copies, waits for them, and re-layouts  2.39 us

profile of v2, /device:TPU:1, one launch (start us, length us, event | category | flops | bytes accessed | tf_op | source)
XLA Modules:
  0.0 84.0 jit_solution(7279973243665960621)
XLA Ops:
  0.6 80.9 %shard_map.50 = (f32[4,2,128,128]{3,2,1,0:T(8,128)}, f32[3]{0:T(128)}) custom-call(s32[16,128]{1,0:T(8,128)} %bitcast.1, s32[3]{0:T(128)} %refs_1_.1, f32[4,2,128,128]{3,2,1,0:T(8,128)} %refs_2_.1), custom_call_target="tpu_custom_call" | custom-call | tf_op jit(solution)/shard_map/pallas_call | solution.py:385
  81.6 0.0 copy-start
  81.6 1.9 %copy.7 = f32[4,2,128,128]{3,2,1,0:T(8,128)} copy(f32[4,2,128,128]{3,2,1,0:T(8,128)} %get-tuple-element.4) | data formatting | bytes 1048576
  83.4 0.0 copy-done
  83.4 0.5 copy.8
Async XLA Ops:
  81.6 1.9 %copy-start = (f32[3]{0:T(128)S(1)}, f32[3]{0:T(128)}, u32[]{:S(2)}) copy-start(f32[3]{0:T(128)} %get-tuple-element.5) | copy-start | bytes 40

commit v3 on v2

--- a/solution.py
+++ b/solution.py
@@ -13,11 +13,12 @@
 SPAN = {"A": (0, 3), "B": (3, 4), "C": (7, 3)}
 TILE = {"A": 0, "B": 1, "C": 2}
 COPIES = (("B", -1), ("B", 1), ("A", -1), ("C", 1), ("A", -2), ("C", 2))
+DOWN_B, UP_B, DOWN_A, UP_C, PASS_A, PASS_C = range(6)
 
 
 def kernel(n_row, n_col, n_layer, cols_ref, signs_ref, blk_ref, out_ref, tr_ref, own, left1, left2, right1, right2, high, low,
-           acc, flip, zero, mine, tb0, tb1, tb2, tb3, gsend, grecv, hsend, hrecv, osend, orecv, zsem, t0s, t0r, t1s, t1r, t2s, t2r,
-           t3s, t3r):
+           acc, flip, zero, mine, tb1, tb2, tb3, gsend, grecv, hsend, hrecv, osend, orecv, zsem, t1s, t1r, t2s, t2r, t3s,
+           t3r):
     row, col, layer = lax.axis_index("row"), lax.axis_index("col"), lax.axis_index("layer")
     i32 = jnp.int32
     core = lax.rem(col, 2)
@@ -38,9 +39,7 @@
 
     peer = {
         1: pick(b == 0, (*here, base + 3), (*up, far + 1)),
-        2: (*up, far + 1 + 2 * b),
         -1: pick(b == 0, (*down, far + 3), (*here, base + 1)),
-        -2: (*down, far + 1 + 2 * b),
     }
     slot_up = jnp.where(first, 0, 1)
     slot_down = jnp.where(last, 1, 0)
@@ -55,8 +54,8 @@
         pltpu.make_async_copy(ref, ref, sem).wait()
 
     others = [(row, col, turn(layer, p, n_layer)) for p in range(1, n_layer)]
-    col_peers = [(row, turn(col, p, n_col), jnp.where(lax.rem(col + p, 2) == 0, 1, 5)) for p in range(1, n_col)]
-    row_peers = [(turn(row, p, n_row), col, base + 1) for p in range(1, n_row)]
+    col_peers = [(row, turn(col, p, n_col), (far if p % 2 else base) + 1 + 2 * b) for p in range(1, n_col)]
+    row_peers = [(turn(row, p, n_row), col, layer) for p in range(1, n_row)]
 
     barrier = pltpu.get_barrier_semaphore()
 
@@ -77,19 +76,9 @@
 
     @pl.when(collector)
     def _():
-        for to in peer.values():
+        for to in [*peer.values(), *col_peers, *row_peers]:
             greet(to)
-        want = 1 + (n_layer - 1) + n_layer + 4
-
-        @pl.when(b == 0)
-        def _():
-            for to in col_peers + row_peers:
-                greet(to)
-            pl.semaphore_wait(barrier, want + (n_col - 1) + (n_row - 1))
-
-        @pl.when(b == 1)
-        def _():
-            pl.semaphore_wait(barrier, want)
+        pl.semaphore_wait(barrier, 1 + (n_layer - 1) + n_layer + 2 + (n_col - 1) + (n_row - 1))
 
     @pl.when(jnp.logical_not(collector))
     def _():
@@ -122,18 +111,19 @@
             pltpu.make_async_copy(zero, out_ref.at[a, 1], zsem.at[a]).start()
 
     def landing(k, t):
-        tile, to = COPIES[k]
-        if to == 2:
+        tile, come = COPIES[k]
+        if come == 2:
             return left2.at[t]
-        if to == -2:
+        if come == -2:
             return right2.at[t]
         start, size = SPAN[tile]
-        return left1.at[t, pl.ds(start - 3, size)] if to == 1 else right1.at[t, pl.ds(start, size)]
+        return left1.at[t, pl.ds(start - 3, size)] if come == 1 else right1.at[t, pl.ds(start, size)]
 
     def copy(k, t):
-        tile, to = COPIES[k]
+        tile, come = COPIES[k]
         start, size = SPAN[tile]
-        return remote(own.at[t, pl.ds(start, size)], landing(k, t), hsend.at[t, k], hrecv.at[t, k], peer[to])
+        src = {PASS_A: landing(DOWN_A, t), PASS_C: landing(UP_C, t)}.get(k, own.at[t, pl.ds(start, size)])
+        return remote(src, landing(k, t), hsend.at[t, k], hrecv.at[t, k], peer[1 if come > 0 else -1])
 
     def await_halo(k, t):
         arrived(landing(k, t), hrecv.at[t, k])
@@ -218,7 +208,7 @@
                 def _():
                     remote(src, dst, send, recv, to).wait_send()
 
-    def share_pair():
+    def share_cols():
         eye = lax.broadcasted_iota(i32, (B, B), 0) == lax.broadcasted_iota(i32, (B, B), 1)
 
         def diagonal(t):
@@ -236,15 +226,7 @@
         norm = jnp.sum(diag + 2.0 * off, axis=0, keepdims=True)
         three = jnp.where(signs_ref[2] == 1, norm, 2.0 * two - norm)
         line = lax.broadcasted_iota(i32, (8, B), 0)
-        mine[...] = jnp.where(line == 0, one, jnp.where(line == 1, two, jnp.where(line == 2, three, 0.0)))
-
-        @pl.when(b == 1)
-        def _():
-            remote(mine, tb0, t0s, t0r, (*here, base + 1)).start()
-
-    def share_cols():
-        arrived(tb0, t0r)
-        tb1[col] = mine[...] + tb0[...]
+        tb1[col] = jnp.where(line == 0, one, jnp.where(line == 1, two, jnp.where(line == 2, three, 0.0)))
         for p, to in enumerate(col_peers):
             remote(tb1.at[col], tb1.at[col], t1s.at[p], t1r.at[col], to).start()
 
@@ -263,13 +245,13 @@
         total = jnp.sum(jnp.sum(tb2[...], axis=0), axis=1, keepdims=True) / (n_row * n_col * ROWS * B)
         mine[...] = jnp.broadcast_to(total, (8, B))
         for p, to in enumerate(others):
-            remote(mine, tb3, t3s.at[p], t3r, to).start()
+            remote(mine, tb3.at[b], t3s.at[p], t3r.at[b], to).start()
 
     @pl.when(collector)
     def _():
         for r, k in ((0, 5), (1, -4), (3, -2), (5, 0)):
             put(r, k, jnp.zeros((B, B), jnp.float32))
-        for tile, ks in (("B", (0, 1)), ("A", (2, 4)), ("C", (3, 5))):
+        for tile, ks in (("C", (UP_C,)), ("A", (DOWN_A,)), ("B", (UP_B, DOWN_B))):
             start, size = SPAN[tile]
             for n in range(start, start + size):
                 arrived(own.at[0, n], grecv.at[n])
@@ -277,15 +259,14 @@
                 copy(k, 0).start()
 
         def step(t, carry):
+            pl.when(t == 2)(share_cols)
             for n, (a, q) in enumerate(BLOCKS):
                 put_both(a, q, own[t, n])
-            pl.when(t == 2)(share_pair)
             acc[0] = product("A", 0, 6)
             acc[1] = product("B", 0, 2)
             acc[2] = product("C", 0, 2)
-            pl.when((t == 2) & (b == 0))(share_cols)
-
-            def after(tile, ks):
+
+            def after(tile, *ks):
                 @pl.when(t < 2)
                 def _():
                     for k in ks:
@@ -295,38 +276,41 @@
                 def _():
                     deliver(tile)
 
-            await_halo(1, t)
-            await_halo(3, t)
-            for n in range(3, 10):
+            await_halo(UP_C, t)
+            copy(PASS_C, t).start()
+            await_halo(DOWN_A, t)
+            copy(PASS_A, t).start()
+            pl.when(t == 2)(share_rows)
+            for n in range(7, 10):
                 a, q = BLOCKS[n]
                 put(q - 2, a - 2, left1[t, n - 3].T)
-            await_halo(0, t)
-            await_halo(2, t)
-            for n in range(7):
+            for n in range(3):
                 a, q = BLOCKS[n]
                 put_both(a + 2, q + 2, right1[t, n])
+            await_halo(UP_B, t)
+            await_halo(DOWN_B, t)
+            for n in range(3, 7):
+                a, q = BLOCKS[n]
+                put(q - 2, a - 2, left1[t, n - 3].T)
+                put_both(a + 2, q + 2, right1[t, n])
             finish(t, "B", acc[1] + product("B", -2, 0) + product("B", 2, 6))
-            after("B", (0, 1))
-            await_halo(5, t)
+            pl.when(t == 2)(share_layers)
+            after("B", UP_B, DOWN_B)
+            await_halo(PASS_C, t)
             for n in range(7, 10):
                 a, q = BLOCKS[n]
                 put(q - 4, a - 4, left2[t, n - 7].T)
             finish(t, "A", acc[0] + product("A", -4, 0))
-            after("A", (2, 4))
-            await_halo(4, t)
+            after("A", DOWN_A)
+            await_halo(PASS_A, t)
             for n in range(3):
                 a, q = BLOCKS[n]
                 put_both(a + 4, q + 4, right2[t, n])
             finish(t, "C", acc[2] + product("C", 2, 6))
-            after("C", (3, 5))
+            after("C", UP_C)
             return carry
 
         lax.fori_loop(0, STEPS, step, 0)
-
-        @pl.when(b == 0)
-        def _():
-            share_rows()
-            share_layers()
 
         for t in range(STEPS):
             for k in range(len(COPIES)):
@@ -334,19 +318,13 @@
         for tile in SPAN:
             delivered(tile)
 
-        @pl.when(b == 0)
-        def _():
-            for p, to in enumerate(col_peers):
-                remote(tb1.at[col], tb1.at[col], t1s.at[p], t1r.at[col], to).wait_send()
-            for p, to in enumerate(row_peers):
-                remote(tb2.at[row], tb2.at[row], t2s.at[p], t2r.at[row], to).wait_send()
-            for p, to in enumerate(others):
-                remote(mine, tb3, t3s.at[p], t3r, to).wait_send()
-            tb3[...] = mine[...]
-
-        @pl.when(b == 1)
-        def _():
-            remote(mine, tb0, t0s, t0r, (*here, base + 1)).wait_send()
+        for p, to in enumerate(col_peers):
+            remote(tb1.at[col], tb1.at[col], t1s.at[p], t1r.at[col], to).wait_send()
+        for p, to in enumerate(row_peers):
+            remote(tb2.at[row], tb2.at[row], t2s.at[p], t2r.at[row], to).wait_send()
+        for p, to in enumerate(others):
+            remote(mine, tb3.at[b], t3s.at[p], t3r.at[b], to).wait_send()
+        tb3[b] = mine[...]
 
     for a in range(ROWS):
         has, block, n, to, local = source(a)
@@ -355,12 +333,13 @@
         def _():
             remote(block, own.at[0, n], gsend.at[a], grecv.at[n], to).wait_send()
 
-    @pl.when(u != 1)
-    def _():
-        arrived(tb3, t3r)
+    for k in range(2):
+        @pl.when(u != 1 + 2 * k)
+        def _():
+            arrived(tb3.at[k], t3r.at[k])
 
     for t in range(STEPS):
-        tr_ref[t] = tb3[t, 0]
+        tr_ref[t] = tb3[0, t, 0] + tb3[1, t, 0]
     for a in range(ROWS):
         arrived(out_ref.at[a, 0], orecv.at[a, 0])
 
@@ -388,7 +367,7 @@
             in_specs=[
                 pl.BlockSpec(memory_space=pltpu.SMEM),
                 pl.BlockSpec(memory_space=pltpu.SMEM),
-                pl.BlockSpec(memory_space=pl.ANY),
+                pl.BlockSpec(memory_space=pltpu.HBM),
             ],
             out_specs=(pl.BlockSpec(memory_space=pl.ANY), pl.BlockSpec(memory_space=pltpu.SMEM)),
             scratch_shapes=[
@@ -403,10 +382,9 @@
                 pltpu.VMEM((10, B, B), f32),
                 pltpu.VMEM((B, B), f32),
                 pltpu.VMEM((8, B), f32),
-                pltpu.VMEM((8, B), f32),
                 pltpu.VMEM((n_col, 8, B), f32),
                 pltpu.VMEM((n_row, 8, B), f32),
-                pltpu.VMEM((8, B), f32),
+                pltpu.VMEM((2, 8, B), f32),
                 dma((ROWS,)),
                 dma((10,)),
                 dma((STEPS, len(COPIES))),
@@ -414,17 +392,15 @@
                 dma((2, 10)),
                 dma((ROWS, 2)),
                 dma((ROWS,)),
-                dma,
-                dma,
                 dma((n_col,)),
                 dma((n_col,)),
                 dma((n_row,)),
                 dma((n_row,)),
                 dma((n_layer,)),
-                dma,
+                dma((2,)),
             ],
             compiler_params=pltpu.CompilerParams(
-                collective_id=0, has_side_effects=True, vmem_limit_bytes=60 * 1024 * 1024
+                collective_id=0, has_side_effects=True, vmem_limit_bytes=48 * 1024 * 1024
             ),
         )(columns.T, signs, blocks)
 

time: 84.1 us -> 72 us (0.86)
  Pallas kernels: 80.9 us -> 67.3 us
  local copies, waits for them, and re-layouts: 2.39 us -> 3.69 us
    pallas_call x1, Pallas kernels: 80.9 us -> 67.3 us  [shards(): pl.pallas_call(body, out_shape=(jax.ShapeDtypeStruct(blocks.shape, f32),...]
    unnamed x4 -> x8, local copies, waits for them, and re-layouts: 2.39 us -> 3.69 us
where the time goes in v3:
time: 72 us; the launch traced here: 71.6 us
  Pallas kernels  67.3 us (93%)
  local copies, waits for them, and re-layouts  3.69 us (5%)
    pallas_call x1, Pallas kernels, shards(): pl.pallas_call(body, out_shape=(jax.ShapeDtypeStruct(blocks.shape, f32),...  67.3 us
    unnamed x8, local copies, waits for them, and re-layouts  3.69 us

profile of v3, /device:TPU:1, one launch (start us, length us, event | category | flops | bytes accessed | tf_op | source)
XLA Modules:
  0.0 71.6 jit_solution(1046791458592005784)
XLA Ops:
  0.6 0.0 copy-start.2
  0.6 0.6 copy-done.2
  1.3 0.0 copy-start
  1.3 1.0 %copy-done = f32[4,2,128,128]{3,2,1,0:T(8,128)S(1)} copy-done((f32[4,2,128,128]{3,2,1,0:T(8,128)S(1)}, f32[4,2,128,128]{3,2,1,0:T(8,128)}, u32[]{:S(2)}) %copy-start) | copy-done | bytes 524312
  2.3 0.0 copy-start.1
  2.3 0.7 copy-done.1
  3.0 67.3 %shard_map.50 = (f32[4,2,128,128]{3,2,1,0:T(8,128)S(1)}, f32[3]{0:T(128)S(1)}) custom-call(s32[16,128]{1,0:T(8,128)S(1)} %bitcast.1, s32[3]{0:T(128)S(1)} %copy-done.2, f32[4,2,128,128]{3,2,1,0:T(8,128)S(1)} %copy-done), custom_call_target="tpu_custom_call" | custom-call | tf_op jit(solution)/shard_map/pallas_call | solution.py:364
  70.3 0.8 %copy.7 = f32[4,2,128,128]{3,2,1,0:T(8,128)} copy(f32[4,2,128,128]{3,2,1,0:T(8,128)S(1)} %get-tuple-element.4) | data formatting | bytes 1048576
  71.1 0.5 copy.8
Async XLA Ops:
  0.6 0.7 copy-start.2
  1.3 1.0 %copy-start = (f32[4,2,128,128]{3,2,1,0:T(8,128)S(1)}, f32[4,2,128,128]{3,2,1,0:T(8,128)}, u32[]{:S(2)}) copy-start(f32[4,2,128,128]{3,2,1,0:T(8,128)} %refs_2_.1) | copy-start | bytes 1572868
  2.3 0.7 copy-start.1

commit v4 on v3

v4 whole, which is shorter than its diff:
```python
import jax
import jax.numpy as jnp
from jax import lax
from jax.experimental import pallas as pl
from jax.experimental.pallas import tpu as pltpu
from jax.sharding import PartitionSpec as P

MESH = pl.DeviceIdType.MESH
B = 128
ROWS = 4
STEPS = 3
BLOCKS = ((0, 0), (0, 1), (1, 1), (0, 2), (0, 3), (1, 2), (1, 3), (-2, 2), (-1, 2), (-1, 3))
SPAN = {"A": (0, 3), "B": (3, 4), "D": (7, 3)}
CORNER = {"A": (0, 0), "B": (0, 2), "D": (-2, 2)}
UP, DOWN = 1, -1


def kernel(n_row, n_col, n_layer, cols_ref, signs_ref, blk_ref, out_ref, tr_ref, own, left, right, high, low, acc,
           flip, zero, mine, tb1, tb2, tb3, gsend, grecv, hsend, hrecv, osend, orecv, zsem, t1s, t1r, t2s, t2r, t3s,
           t3r):
    row, col, layer = lax.axis_index("row"), lax.axis_index("col"), lax.axis_index("layer")
    i32 = jnp.int32
    core = lax.rem(col, 2)
    base = 4 * core
    u = jnp.where(layer < base, layer - base + n_layer, layer - base)
    collector = (u == 1) | (u == 3)
    b = jnp.where(u == 3, 1, 0)
    first = (row == 0) & (col == 0)
    last = (row == n_row - 1) & (col == n_col - 1)
    wrap_up, wrap_down = col == n_col - 1, col == 0
    up = (jnp.where(wrap_up, jnp.where(row == n_row - 1, 0, row + 1), row), jnp.where(wrap_up, 0, col + 1))
    down = (jnp.where(wrap_down, jnp.where(row == 0, n_row - 1, row - 1), row), jnp.where(wrap_down, n_col - 1, col - 1))
    here = (row, col)
    far = 4 - base

    def pick(cond, x, y):
        return tuple(jnp.where(cond, p, q) for p, q in zip(x, y))

    peer = {
        1: pick(b == 0, (*here, base + 3), (*up, far + 1)),
        -1: pick(b == 0, (*down, far + 3), (*here, base + 1)),
    }
    slot_up = jnp.where(first, 0, 1)
    slot_up_before = jnp.where((row == 0) & (col == 1), 0, 1)
    slot_down = jnp.where(first, 1, 0)
    slot_down_after = jnp.where(last, 1, 0)

    def turn(x, p, n):
        return jnp.where(x + p >= n, x + p - n, x + p)

    def remote(src, dst, send, recv, to):
        return pltpu.make_async_remote_copy(src, dst, send, recv, device_id=to, device_id_type=MESH)

    def arrived(ref, sem):
        pltpu.make_async_copy(ref, ref, sem).wait()

    others = [(row, col, turn(layer, p, n_layer)) for p in range(1, n_layer)]
    col_peers = [(row, turn(col, p, n_col), (far if p % 2 else base) + 1 + 2 * b) for p in range(1, n_col)]
    row_peers = [(turn(row, p, n_row), col, layer) for p in range(1, n_row)]

    barrier = pltpu.get_barrier_semaphore()

    def greet(to):
        pl.semaphore_signal(barrier, inc=1, device_id=to, device_id_type=MESH)

    def ready(group, start, columns):
        for k in columns:
            greet((*group, turn(start, k, n_layer)))

    @pl.when(u == 1)
    def _():
        ready(here, base, (0, 2, 3))
        ready(down, far, (2, 3, 4, 5, 6, 7))
        ready(up, far, (4, 5, 6, 7))

    @pl.when(u == 3)
    def _():
        ready(here, base, (0, 1, 2, 4, 5))
        ready(down, far, (6, 7))
        ready(up, far, (0, 1, 6, 7))

    for k in range(2):
        @pl.when(u != 1 + 2 * k)
        def _():
            greet((*here, base + 1 + 2 * k))

    greet((*down, far + 3))
    greet((*up, far + 1))

    @pl.when(collector)
    def _():
        for to in [*peer.values(), *col_peers, *row_peers]:
            greet(to)
        pl.semaphore_wait(barrier, 2 + (n_layer - 1) + n_layer + 2 + (n_col - 1) + (n_row - 1))

    @pl.when(jnp.logical_not(collector) & (u < 6))
    def _():
        pl.semaphore_wait(barrier, 3)

    @pl.when(u >= 6)
    def _():
        pl.semaphore_wait(barrier, 4)

    def sources(a):
        pair, d, q = a // 2, u - a, u - 2 * (a // 2)
        two, four = jnp.where(q >= 2, 1, 0), jnp.where(q >= 4, 1, 0)
        n = q + 1 + 2 * two + four if a % 2 else q + two + 2 * four
        has = (d >= 0) & (d <= ROWS)
        block = blk_ref.at[a, jnp.where(d == ROWS, slot_up, 0)]
        mine_, next_ = (*here, base + 1 + 2 * pair), ((*here, base + 3) if a < 2 else (*up, far + 1))
        third = (*up, far + 1) if a < 2 else (*up, far + 3)
        yield has & (q < 2), block, right.at[0, n], grecv.at[2, n], (*down, far + 3) if a < 2 else (*here, base + 1), False
        yield has, block, left.at[0, n], grecv.at[1, n], pick(q >= 4, third, next_), u == 3 if a < 2 else False
        yield has, block, own.at[0, n], grecv.at[0, n], pick(q >= 4, next_, mine_), u == 1 + 2 * pair
        c = jnp.where(u < ROWS, u, u - n_layer) - 2 * pair + 2
        n = jnp.where(c >= 0, 3 + a % 2 + 2 * c, 9 + a % 2 + c)
        has = (u >= a + ROWS) | (u < 2) if a >= 2 else u >= a + ROWS
        block = blk_ref.at[a, jnp.where(u == a + ROWS, slot_down, 0)]
        yield has, block, right.at[0, n], grecv.at[2, n], (*down, far + 1 + 2 * pair), False

    plans = list(zip(*(sources(a) for a in range(ROWS))))
    for k, plan in enumerate(plans):
        for a, (has, block, dst, sem, to, local) in enumerate(plan):
            @pl.when(has & jnp.logical_not(local))
            def _():
                remote(block, dst, gsend.at[k, a], sem, to).start()

            if local is not False:
                @pl.when(has & local)
                def _():
                    pltpu.make_async_copy(block, dst, sem).start()

    zero[...] = jnp.zeros_like(zero)
    for a in range(ROWS):
        @pl.when(u != a + ROWS)
        def _():
            pltpu.make_async_copy(zero, out_ref.at[a, 1], zsem.at[a]).start()

    def copy(tile, way, t):
        part = pl.ds(*SPAN[tile])
        k = 2 * list(SPAN).index(tile) + (way == UP)
        dst = left if way == UP else right
        return remote(own.at[t, part], dst.at[t, part], hsend.at[t, k], hrecv.at[t, k], peer[way])

    def come(tile, way, t):
        part = pl.ds(*SPAN[tile])
        k = 2 * list(SPAN).index(tile) + (way == UP)
        dst = left if way == UP else right
        blocks = range(SPAN[tile][0], sum(SPAN[tile]))
        turned = way == DOWN and tile != "A"

        @pl.when(t == 0)
        def _():
            for n in blocks:
                arrived(dst.at[0, n], grecv.at[1 if way == UP else 2, n])
            if turned:
                for n in blocks:
                    a, q = BLOCKS[n]
                    put(a + 2, q + 2, dst[0, n].T)

        @pl.when(t > 0)
        def _():
            arrived(dst.at[t, part], hrecv.at[t, k])
            if turned:
                for n in blocks:
                    a, q = BLOCKS[n]
                    put(a + 2, q + 2, dst[t, n])

        if not turned:
            for n in blocks:
                a, q = BLOCKS[n]
                put_both(a - 2 * way, q - 2 * way, dst[t, n])

    def put(r, k, x):
        h = x.astype(jnp.bfloat16)
        lo = (x - h.astype(jnp.float32)).astype(jnp.bfloat16)
        high[(r + 2) * B:(r + 3) * B, (k + 4) * B:(k + 5) * B] = h
        low[(r + 2) * B:(r + 3) * B, (k + 4) * B:(k + 5) * B] = lo

    def put_both(r, k, x):
        if -2 <= r < 4:
            put(r, k, x)
        if k > r and -2 <= k < 4:
            put(k, r, x.T)

    def product(tile, start, stop):
        i, j = CORNER[tile]

        def part(ref, r):
            return ref[(r + 2) * B:(r + 4) * B, (start + 4) * B:(stop + 4) * B]

        def dot(x, y):
            return lax.dot_general(x, y, (((1,), (1,)), ((), ())), preferred_element_type=jnp.float32)

        ah, al, bh, bl = part(high, i), part(low, i), part(high, j), part(low, j)
        return dot(ah, bh) + (dot(al, bh) + dot(ah, bl))

    def there(a, q):
        at_row = ROWS * (row * n_col + col) + 2 * b + a
        at_col = at_row + q - a
        slot = 2 * turn(base + 2 * b, q, n_layer)
        r = jnp.maximum(at_row, 0)
        return (at_row >= 0) & ((cols_ref[slot, r] == at_col) | (cols_ref[slot + 1, r] == at_col))

    def finish(t, tile, total, masks):
        square = signs_ref[t] == 1
        keep = jnp.where(square, 0.0, 2.0).astype(jnp.float32)
        sign = jnp.where(square, 1.0, -1.0).astype(jnp.float32)
        start, size = SPAN[tile]
        for n in range(start, start + size):
            a, q = BLOCKS[n]
            factor = sign * masks[n]
            part = total[(a % 2) * B:(a % 2 + 1) * B, (q % 2) * B:(q % 2 + 1) * B]
            own[t + 1, n] = keep * own[t, n] + factor * part

    def results(tile):
        start, size = SPAN[tile]
        for n in range(start, start + size):
            a, q = BLOCKS[n]
            wide = q - a == ROWS
            at_a, at_q = turn(base + 2 * b, a % n_layer, n_layer), turn(base + 2 * b, q, n_layer)
            if a >= 0:
                group, r, slot = here, 2 * b + a, 0
            else:
                group = pick(b == 0, down, here)
                r = jnp.where(b == 0, ROWS + a, 2 + a)
                slot = jnp.where(b == 0, slot_up_before, slot_up) if wide else 0
            yield own.at[STEPS, n], out_ref.at[r, slot], osend.at[0, n], orecv.at[r, slot], (*group, at_q), q == 1
            if q > a:
                over = 2 * b + q >= ROWS
                group = pick(over, up, here)
                r = jnp.where(over, 2 * b + q - ROWS, 2 * b + q)
                slot = jnp.where(over, slot_down_after, slot_down) if wide else 0
                local = b == 0 if a == 1 else False
                yield flip.at[n], out_ref.at[r, slot], osend.at[1, n], orecv.at[r, slot], (*group, at_a), local

    def deliver(tile):
        start, size = SPAN[tile]
        for n in range(start, start + size):
            a, q = BLOCKS[n]
            if q > a:
                flip[n] = own[STEPS, n].T
        for src, dst, send, recv, to, local in results(tile):
            if local is not True:
                @pl.when(jnp.logical_not(local))
                def _():
                    remote(src, dst, send, recv, to).start()
            if local is not False:
                @pl.when(local)
                def _():
                    pltpu.make_async_copy(src, dst, recv).start()

    def delivered(tile):
        for src, dst, send, recv, to, local in results(tile):
            if local is not True:
                @pl.when(jnp.logical_not(local))
                def _():
                    remote(src, dst, send, recv, to).wait_send()

    def share_cols():
        eye = lax.broadcasted_iota(i32, (B, B), 0) == lax.broadcasted_iota(i32, (B, B), 1)

        def diagonal(t):
            return jnp.sum(jnp.where(eye, own[t, 0] + own[t, 2], 0.0), axis=0, keepdims=True)

        one, two = diagonal(1), diagonal(2)
        diag = jnp.zeros((B, B), jnp.float32)
        off = jnp.zeros((B, B), jnp.float32)
        for n, (a, q) in enumerate(BLOCKS):
            x = own[2, n]
            if q > a:
                off = off + x * x
            else:
                diag = diag + x * x
        norm = jnp.sum(diag + 2.0 * off, axis=0, keepdims=True)
        three = jnp.where(signs_ref[2] == 1, norm, 2.0 * two - norm)
        line = lax.broadcasted_iota(i32, (8, B), 0)
        tb1[col] = jnp.where(line == 0, one, jnp.where(line == 1, two, jnp.where(line == 2, three, 0.0)))
        for p, to in enumerate(col_peers):
            remote(tb1.at[col], tb1.at[col], t1s.at[p], t1r.at[col], to).start()

    def share_rows():
        for p in range(1, n_col):
            c = turn(col, p, n_col)
            arrived(tb1.at[c], t1r.at[c])
        tb2[row] = jnp.sum(tb1[...], axis=0)
        for p, to in enumerate(row_peers):
            remote(tb2.at[row], tb2.at[row], t2s.at[p], t2r.at[row], to).start()

    def share_layers():
        for p in range(1, n_row):
            r = turn(row, p, n_row)
            arrived(tb2.at[r], t2r.at[r])
        total = jnp.sum(jnp.sum(tb2[...], axis=0), axis=1, keepdims=True) / (n_row * n_col * ROWS * B)
        mine[...] = jnp.broadcast_to(total, (8, B))
        for p, to in enumerate(others):
            remote(mine, tb3.at[b], t3s.at[p], t3r.at[b], to).start()

    @pl.when(collector)
    def _():
        for r, k in ((0, 5), (1, -4), (3, -2), (-2, 3)):
            put(r, k, jnp.zeros((B, B), jnp.float32))
        masks = [jnp.where(there(a, q), 1.0, 0.0).astype(jnp.float32) for a, q in BLOCKS]

        for n in range(len(BLOCKS)):
            arrived(own.at[0, n], grecv.at[0, n])

        def step(t, carry):
            pl.when(t == 2)(share_cols)
            for n, (a, q) in enumerate(BLOCKS):
                put_both(a, q, own[t, n])
            acc[0] = product("A", 0, 4)
            acc[1] = product("B", 0, 2)

            def send(when, *copies):
                @pl.when(when)
                def _():
                    for tile, way in copies:
                        copy(tile, way, t + 1).start()

            def make_d(even):
                come("A", DOWN, t)
                come("A", UP, t)
                if even:
                    pl.when(t == 2)(share_rows)
                finish(t, "D", product("D", -2, 4), masks)
                if even:
                    send(t == 0, ("D", UP), ("D", DOWN))
                    pl.when(t == 2)(lambda: deliver("D"))
                else:
                    copy("D", DOWN, 2).start()

            come("B", UP, t)
            pl.when(t != 1)(lambda: make_d(True))
            come("D", DOWN, t)
            come("D", UP, t)
            finish(t, "A", acc[0] + product("A", -4, 0) + product("A", 4, 6), masks)
            send(t < 2, ("A", DOWN))
            send(t == 1, ("A", UP))
            pl.when(t == 2)(lambda: deliver("A"))
            pl.when(t == 1)(lambda: make_d(False))
            come("B", DOWN, t)
            finish(t, "B", acc[1] + product("B", -2, 0) + product("B", 2, 6), masks)
            send(t < 2, ("B", UP), ("B", DOWN))
            send(t == 0, ("A", UP))
            send(t == 1, ("D", UP))

            @pl.when(t == 2)
            def _():
                share_layers()
                deliver("B")

            return carry

        lax.fori_loop(0, STEPS, step, 0)

        for t in range(1, STEPS):
            for tile in SPAN:
                for way in (UP, DOWN):
                    copy(tile, way, t).wait_send()
        for tile in SPAN:
            delivered(tile)

        for p, to in enumerate(col_peers):
            remote(tb1.at[col], tb1.at[col], t1s.at[p], t1r.at[col], to).wait_send()
        for p, to in enumerate(row_peers):
            remote(tb2.at[row], tb2.at[row], t2s.at[p], t2r.at[row], to).wait_send()
        for p, to in enumerate(others):
            remote(mine, tb3.at[b], t3s.at[p], t3r.at[b], to).wait_send()
        tb3[b] = mine[...]

    for k, plan in enumerate(plans):
        for a, (has, block, dst, sem, to, local) in enumerate(plan):
            @pl.when(has & jnp.logical_not(local))
            def _():
                remote(block, dst, gsend.at[k, a], sem, to).wait_send()

    for k in range(2):
        @pl.when(u != 1 + 2 * k)
        def _():
            arrived(tb3.at[k], t3r.at[k])

    for t in range(STEPS):
        tr_ref[t] = tb3[0, t, 0] + tb3[1, t, 0]
    for a in range(ROWS):
        arrived(out_ref.at[a, 0], orecv.at[a, 0])

        @pl.when(u == a + ROWS)
        def _():
            arrived(out_ref.at[a, 1], orecv.at[a, 1])

        @pl.when(u != a + ROWS)
        def _():
            pltpu.make_async_copy(zero, out_ref.at[a, 1], zsem.at[a]).wait()


def solution(mesh):
    n_row, n_col, n_layer = (mesh.shape[name] for name in ("row", "col", "layer"))
    dma = pltpu.SemaphoreType.DMA

    def shards(blocks, columns, signs):
        def body(*refs):
            kernel(n_row, n_col, n_layer, *refs)

        f32, bf16 = jnp.float32, jnp.bfloat16
        return pl.pallas_call(
            body,
            out_shape=(jax.ShapeDtypeStruct(blocks.shape, f32), jax.ShapeDtypeStruct((STEPS,), f32)),
            in_specs=[
                pl.BlockSpec(memory_space=pltpu.SMEM),
                pl.BlockSpec(memory_space=pltpu.SMEM),
                pl.BlockSpec(memory_space=pltpu.HBM),
            ],
            out_specs=(pl.BlockSpec(memory_space=pl.ANY), pl.BlockSpec(memory_space=pltpu.SMEM)),
            scratch_shapes=[
                pltpu.VMEM((STEPS + 1, 10, B, B), f32),
                pltpu.VMEM((STEPS, 10, B, B), f32),
                pltpu.VMEM((STEPS, 10, B, B), f32),
                pltpu.VMEM((6 * B, 10 * B), bf16),
                pltpu.VMEM((6 * B, 10 * B), bf16),
                pltpu.VMEM((2, 2 * B, 2 * B), f32),
                pltpu.VMEM((10, B, B), f32),
                pltpu.VMEM((B, B), f32),
                pltpu.VMEM((8, B), f32),
                pltpu.VMEM((n_col, 8, B), f32),
                pltpu.VMEM((n_row, 8, B), f32),
                pltpu.VMEM((2, 8, B), f32),
                dma((4, ROWS)),
                dma((3, 10)),
                dma((STEPS, 6)),
                dma((STEPS, 6)),
                dma((2, 10)),
                dma((ROWS, 2)),
                dma((ROWS,)),
                dma((n_col,)),
                dma((n_col,)),
                dma((n_row,)),
                dma((n_row,)),
                dma((n_layer,)),
                dma((2,)),
            ],
            compiler_params=pltpu.CompilerParams(
                collective_id=0, has_side_effects=True, vmem_limit_bytes=60 * 1024 * 1024
            ),
        )(columns.T, signs, blocks)

    return jax.shard_map(
        shards,
        mesh=mesh,
        in_specs=(P(("row", "col"), "layer", None, None), P(), P()),
        out_specs=(P(("row", "col"), "layer", None, None), P()),
        check_vma=False,
    )
```

time: 72 us -> 59.1 us (0.82)
  the two profiles are of different devices: /device:TPU:1 before, /device:TPU:6 now
where the time goes in v4:
time: 59.1 us; the launch traced here: 58.9 us
  Pallas kernels  55.9 us (95%)
  local copies, waits for them, and re-layouts  2.39 us (4%)
  between operations  0.65 us (1%)
    pallas_call x1, Pallas kernels, shards(): pl.pallas_call(body, out_shape=(jax.ShapeDtypeStruct(blocks.shape, f32),...  55.9 us
    unnamed x4, local copies, waits for them, and re-layouts  2.39 us

profile of v4, /device:TPU:6, one launch (start us, length us, event | category | flops | bytes accessed | tf_op | source)
XLA Modules:
  0.0 58.9 jit_solution(13005588299676664469)
XLA Ops:
  0.6 55.9 %shard_map.50 = (f32[4,2,128,128]{3,2,1,0:T(8,128)}, f32[3]{0:T(128)}) custom-call(s32[16,128]{1,0:T(8,128)} %bitcast.1, s32[3]{0:T(128)} %refs_1_.1, f32[4,2,128,128]{3,2,1,0:T(8,128)} %refs_2_.1), custom_call_target="tpu_custom_call" | custom-call | tf_op jit(solution)/shard_map/pallas_call | solution.py:406
  56.5 0.0 copy-start
  56.5 1.9 %copy.7 = f32[4,2,128,128]{3,2,1,0:T(8,128)} copy(f32[4,2,128,128]{3,2,1,0:T(8,128)} %get-tuple-element.4) | data formatting | bytes 1048576
  58.4 0.0 copy-done
  58.4 0.5 copy.8
Async XLA Ops:
  56.5 1.9 %copy-start = (f32[3]{0:T(128)S(1)}, f32[3]{0:T(128)}, u32[]{:S(2)}) copy-start(f32[3]{0:T(128)} %get-tuple-element.5) | copy-start | bytes 40

commit v5 on v4

--- a/solution.py
+++ b/solution.py
@@ -16,8 +16,8 @@
 
 
 def kernel(n_row, n_col, n_layer, cols_ref, signs_ref, blk_ref, out_ref, tr_ref, own, left, right, high, low, acc,
-           flip, zero, mine, tb1, tb2, tb3, gsend, grecv, hsend, hrecv, osend, orecv, zsem, t1s, t1r, t2s, t2r, t3s,
-           t3r):
+           flip, zero, mine, tb0, tb1, tb2, tb3, gsend, grecv, hsend, hrecv, osend, orecv, zsem, t0s, t0r, t1s, t1r, t2s, t2r,
+           t3s, t3r):
     row, col, layer = lax.axis_index("row"), lax.axis_index("col"), lax.axis_index("layer")
     i32 = jnp.int32
     core = lax.rem(col, 2)
@@ -55,7 +55,8 @@
         pltpu.make_async_copy(ref, ref, sem).wait()
 
     others = [(row, col, turn(layer, p, n_layer)) for p in range(1, n_layer)]
-    col_peers = [(row, turn(col, p, n_col), (far if p % 2 else base) + 1 + 2 * b) for p in range(1, n_col)]
+    adder = layer == 0
+    col_peers = [(row, turn(col, p, n_col), layer) for p in range(1, n_col)]
     row_peers = [(turn(row, p, n_row), col, layer) for p in range(1, n_row)]
 
     barrier = pltpu.get_barrier_semaphore()
@@ -87,13 +88,23 @@
     greet((*down, far + 3))
     greet((*up, far + 1))
 
+    @pl.when(jnp.logical_not(adder))
+    def _():
+        greet((*here, 0))
+
     @pl.when(collector)
     def _():
-        for to in [*peer.values(), *col_peers, *row_peers]:
+        for to in peer.values():
             greet(to)
-        pl.semaphore_wait(barrier, 2 + (n_layer - 1) + n_layer + 2 + (n_col - 1) + (n_row - 1))
-
-    @pl.when(jnp.logical_not(collector) & (u < 6))
+        pl.semaphore_wait(barrier, 2 + (n_layer - 1) + n_layer + 2)
+
+    @pl.when(adder)
+    def _():
+        for to in [*col_peers, *row_peers]:
+            greet(to)
+        pl.semaphore_wait(barrier, 3 + (n_layer - 1) + (n_col - 1) + (n_row - 1))
+
+    @pl.when(jnp.logical_not(collector | adder) & (u < 6))
     def _():
         pl.semaphore_wait(barrier, 3)
 
@@ -257,7 +268,7 @@
                 def _():
                     remote(src, dst, send, recv, to).wait_send()
 
-    def share_cols():
+    def share():
         eye = lax.broadcasted_iota(i32, (B, B), 0) == lax.broadcasted_iota(i32, (B, B), 1)
 
         def diagonal(t):
@@ -275,26 +286,36 @@
         norm = jnp.sum(diag + 2.0 * off, axis=0, keepdims=True)
         three = jnp.where(signs_ref[2] == 1, norm, 2.0 * two - norm)
         line = lax.broadcasted_iota(i32, (8, B), 0)
-        tb1[col] = jnp.where(line == 0, one, jnp.where(line == 1, two, jnp.where(line == 2, three, 0.0)))
+        mine[...] = jnp.where(line == 0, one, jnp.where(line == 1, two, jnp.where(line == 2, three, 0.0)))
+        remote(mine, tb0.at[b], t0s, t0r.at[b], (*here, 0)).start()
+
+    @pl.when(adder)
+    def _():
+        for k in range(2):
+            arrived(tb0.at[k], t0r.at[k])
+        tb1[col] = tb0[0] + tb0[1]
         for p, to in enumerate(col_peers):
             remote(tb1.at[col], tb1.at[col], t1s.at[p], t1r.at[col], to).start()
-
-    def share_rows():
         for p in range(1, n_col):
             c = turn(col, p, n_col)
             arrived(tb1.at[c], t1r.at[c])
         tb2[row] = jnp.sum(tb1[...], axis=0)
         for p, to in enumerate(row_peers):
             remote(tb2.at[row], tb2.at[row], t2s.at[p], t2r.at[row], to).start()
-
-    def share_layers():
         for p in range(1, n_row):
             r = turn(row, p, n_row)
             arrived(tb2.at[r], t2r.at[r])
         total = jnp.sum(jnp.sum(tb2[...], axis=0), axis=1, keepdims=True) / (n_row * n_col * ROWS * B)
         mine[...] = jnp.broadcast_to(total, (8, B))
         for p, to in enumerate(others):
-            remote(mine, tb3.at[b], t3s.at[p], t3r.at[b], to).start()
+            remote(mine, tb3, t3s.at[p], t3r, to).start()
+        tb3[...] = mine[...]
+        for p, to in enumerate(col_peers):
+            remote(tb1.at[col], tb1.at[col], t1s.at[p], t1r.at[col], to).wait_send()
+        for p, to in enumerate(row_peers):
+            remote(tb2.at[row], tb2.at[row], t2s.at[p], t2r.at[row], to).wait_send()
+        for p, to in enumerate(others):
+            remote(mine, tb3, t3s.at[p], t3r, to).wait_send()
 
     @pl.when(collector)
     def _():
@@ -306,7 +327,7 @@
             arrived(own.at[0, n], grecv.at[0, n])
 
         def step(t, carry):
-            pl.when(t == 2)(share_cols)
+            pl.when(t == 2)(share)
             for n, (a, q) in enumerate(BLOCKS):
                 put_both(a, q, own[t, n])
             acc[0] = product("A", 0, 4)
@@ -321,8 +342,6 @@
             def make_d(even):
                 come("A", DOWN, t)
                 come("A", UP, t)
-                if even:
-                    pl.when(t == 2)(share_rows)
                 finish(t, "D", product("D", -2, 4), masks)
                 if even:
                     send(t == 0, ("D", UP), ("D", DOWN))
@@ -345,11 +364,7 @@
             send(t == 0, ("A", UP))
             send(t == 1, ("D", UP))
 
-            @pl.when(t == 2)
-            def _():
-                share_layers()
-                deliver("B")
-
+            pl.when(t == 2)(lambda: deliver("B"))
             return carry
 
         lax.fori_loop(0, STEPS, step, 0)
@@ -361,13 +376,7 @@
         for tile in SPAN:
             delivered(tile)
 
-        for p, to in enumerate(col_peers):
-            remote(tb1.at[col], tb1.at[col], t1s.at[p], t1r.at[col], to).wait_send()
-        for p, to in enumerate(row_peers):
-            remote(tb2.at[row], tb2.at[row], t2s.at[p], t2r.at[row], to).wait_send()
-        for p, to in enumerate(others):
-            remote(mine, tb3.at[b], t3s.at[p], t3r.at[b], to).wait_send()
-        tb3[b] = mine[...]
+        remote(mine, tb0.at[b], t0s, t0r.at[b], (*here, 0)).wait_send()
 
     for k, plan in enumerate(plans):
         for a, (has, block, dst, sem, to, local) in enumerate(plan):
@@ -375,13 +384,12 @@
             def _():
                 remote(block, dst, gsend.at[k, a], sem, to).wait_send()
 
-    for k in range(2):
-        @pl.when(u != 1 + 2 * k)
-        def _():
-            arrived(tb3.at[k], t3r.at[k])
+    @pl.when(jnp.logical_not(adder))
+    def _():
+        arrived(tb3, t3r)
 
     for t in range(STEPS):
-        tr_ref[t] = tb3[0, t, 0] + tb3[1, t, 0]
+        tr_ref[t] = tb3[t, 0]
     for a in range(ROWS):
         arrived(out_ref.at[a, 0], orecv.at[a, 0])
 
@@ -422,9 +430,10 @@
                 pltpu.VMEM((10, B, B), f32),
                 pltpu.VMEM((B, B), f32),
                 pltpu.VMEM((8, B), f32),
+                pltpu.VMEM((2, 8, B), f32),
                 pltpu.VMEM((n_col, 8, B), f32),
                 pltpu.VMEM((n_row, 8, B), f32),
-                pltpu.VMEM((2, 8, B), f32),
+                pltpu.VMEM((8, B), f32),
                 dma((4, ROWS)),
                 dma((3, 10)),
                 dma((STEPS, 6)),
@@ -432,12 +441,14 @@
                 dma((2, 10)),
                 dma((ROWS, 2)),
                 dma((ROWS,)),
+                dma,
+                dma((2,)),
                 dma((n_col,)),
                 dma((n_col,)),
                 dma((n_row,)),
                 dma((n_row,)),
                 dma((n_layer,)),
-                dma((2,)),
+                dma,
             ],
             compiler_params=pltpu.CompilerParams(
                 collective_id=0, has_side_effects=True, vmem_limit_bytes=60 * 1024 * 1024

time: 59.1 us -> 55.9 us (0.946)
  the two profiles are of different devices: /device:TPU:6 before, /device:TPU:1 now
where the time goes in v5:
time: 55.9 us; the launch traced here: 55.1 us
  Pallas kernels  52.1 us (93%)
  local copies, waits for them, and re-layouts  2.39 us (4%)
  between operations  0.65 us (1%)
    pallas_call x1, Pallas kernels, shards(): pl.pallas_call(body, out_shape=(jax.ShapeDtypeStruct(blocks.shape, f32),...  52.1 us
    unnamed x4, local copies, waits for them, and re-layouts  2.39 us

profile of v5, /device:TPU:1, one launch (start us, length us, event | category | flops | bytes accessed | tf_op | source)
XLA Modules:
  0.0 55.1 jit_solution(3618674535900302018)
XLA Ops:
  0.6 52.1 %shard_map.50 = (f32[4,2,128,128]{3,2,1,0:T(8,128)}, f32[3]{0:T(128)}) custom-call(s32[16,128]{1,0:T(8,128)} %bitcast.1, s32[3]{0:T(128)} %refs_1_.1, f32[4,2,128,128]{3,2,1,0:T(8,128)} %refs_2_.1), custom_call_target="tpu_custom_call" | custom-call | tf_op jit(solution)/shard_map/pallas_call | solution.py:414
  52.7 0.0 copy-start
  52.7 1.9 %copy.7 = f32[4,2,128,128]{3,2,1,0:T(8,128)} copy(f32[4,2,128,128]{3,2,1,0:T(8,128)} %get-tuple-element.4) | data formatting | bytes 1048576
  54.6 0.0 copy-done
  54.6 0.5 copy.8
Async XLA Ops:
  52.7 1.9 %copy-start = (f32[3]{0:T(128)S(1)}, f32[3]{0:T(128)}, u32[]{:S(2)}) copy-start(f32[3]{0:T(128)} %get-tuple-element.5) | copy-start | bytes 40

commit v6 on v5

--- a/solution.py
+++ b/solution.py
@@ -351,20 +351,36 @@
 
             come("B", UP, t)
             pl.when(t != 1)(lambda: make_d(True))
+            def make_a():
+                finish(t, "A", acc[0] + product("A", -4, 0) + product("A", 4, 6), masks)
+
+            def make_b():
+                come("B", DOWN, t)
+                finish(t, "B", acc[1] + product("B", -2, 0) + product("B", 2, 6), masks)
+
             come("D", DOWN, t)
-            come("D", UP, t)
-            finish(t, "A", acc[0] + product("A", -4, 0) + product("A", 4, 6), masks)
-            send(t < 2, ("A", DOWN))
-            send(t == 1, ("A", UP))
-            pl.when(t == 2)(lambda: deliver("A"))
-            pl.when(t == 1)(lambda: make_d(False))
-            come("B", DOWN, t)
-            finish(t, "B", acc[1] + product("B", -2, 0) + product("B", 2, 6), masks)
-            send(t < 2, ("B", UP), ("B", DOWN))
-            send(t == 0, ("A", UP))
-            send(t == 1, ("D", UP))
-
-            pl.when(t == 2)(lambda: deliver("B"))
+
+            @pl.when(t < 2)
+            def _():
+                come("D", UP, t)
+                make_a()
+                copy("A", DOWN, t + 1).start()
+                send(t == 1, ("A", UP))
+                pl.when(t == 1)(lambda: make_d(False))
+                make_b()
+                copy("B", UP, t + 1).start()
+                copy("B", DOWN, t + 1).start()
+                send(t == 0, ("A", UP))
+                send(t == 1, ("D", UP))
+
+            @pl.when(t == 2)
+            def _():
+                make_b()
+                deliver("B")
+                come("D", UP, t)
+                make_a()
+                deliver("A")
+
             return carry
 
         lax.fori_loop(0, STEPS, step, 0)
@@ -402,6 +418,12 @@
             pltpu.make_async_copy(zero, out_ref.at[a, 1], zsem.at[a]).wait()
 
 
+def hand_over(out_ref, tr_ref, result_ref, traces_ref):
+    result_ref[...] = out_ref[...]
+    for t in range(STEPS):
+        traces_ref[t] = tr_ref[t]
+
+
 def solution(mesh):
     n_row, n_col, n_layer = (mesh.shape[name] for name in ("row", "col", "layer"))
     dma = pltpu.SemaphoreType.DMA
@@ -411,7 +433,7 @@
             kernel(n_row, n_col, n_layer, *refs)
 
         f32, bf16 = jnp.float32, jnp.bfloat16
-        return pl.pallas_call(
+        out, traces = pl.pallas_call(
             body,
             out_shape=(jax.ShapeDtypeStruct(blocks.shape, f32), jax.ShapeDtypeStruct((STEPS,), f32)),
             in_specs=[
@@ -454,6 +476,15 @@
                 collective_id=0, has_side_effects=True, vmem_limit_bytes=60 * 1024 * 1024
             ),
         )(columns.T, signs, blocks)
+        half = pl.BlockSpec((ROWS // 2, 2, B, B), lambda i: (i, 0, 0, 0))
+        return pl.pallas_call(
+            hand_over,
+            grid=(2,),
+            out_shape=(jax.ShapeDtypeStruct(blocks.shape, f32), jax.ShapeDtypeStruct((STEPS,), f32)),
+            in_specs=[half, pl.BlockSpec(memory_space=pltpu.SMEM)],
+            out_specs=(half, pl.BlockSpec(memory_space=pltpu.SMEM)),
+            compiler_params=pltpu.CompilerParams(vmem_limit_bytes=60 * 1024 * 1024),
+        )(out, traces)
 
     return jax.shard_map(
         shards,

time: 55.9 us -> 55.2 us (0.987)
  local copies, waits for them, and re-layouts: 2.39 us -> 0 us
  Pallas kernels: 52.1 us -> 53.9 us
    unnamed x4 -> x0, local copies, waits for them, and re-layouts: 2.39 us -> none
    pallas_call x0 -> x1, Pallas kernels: none -> 1.78 us  [shards(): pl.pallas_call(hand_over, grid=(2,), out_shape=(jax.ShapeDtypeStruct(bloc...]
where the time goes in v6:
time: 55.2 us; the launch traced here: 54.5 us
  Pallas kernels  53.9 us (98%)
  between operations  0.64 us (1%)
    pallas_call x1, Pallas kernels, shards(): pl.pallas_call(body, out_shape=(jax.ShapeDtypeStruct(blocks.shape, f32),...  52.1 us
    pallas_call x1, Pallas kernels, shards(): pl.pallas_call(hand_over, grid=(2,), out_shape=(jax.ShapeDtypeStruct(bloc...  1.78 us

profile of v6, /device:TPU:1, one launch (start us, length us, event | category | flops | bytes accessed | tf_op | source)
XLA Modules:
  0.0 54.5 jit_solution(10672749590327514591)
XLA Ops:
  0.6 52.1 %shard_map.50 = (f32[4,2,128,128]{3,2,1,0:T(8,128)}, f32[3]{0:T(128)}) custom-call(s32[16,128]{1,0:T(8,128)} %bitcast.1, s32[3]{0:T(128)} %refs_1_.1, f32[4,2,128,128]{3,2,1,0:T(8,128)} %refs_2_.1), custom_call_target="tpu_custom_call" | custom-call | tf_op jit(solution)/shard_map/pallas_call | solution.py:436
  52.7 1.8 %shard_map.51 = (f32[4,2,128,128]{3,2,1,0:T(8,128)}, f32[3]{0:T(128)}) custom-call(f32[4,2,128,128]{3,2,1,0:T(8,128)} %get-tuple-element.4.out_ref, f32[3]{0:T(128)} %get-tuple-element.5.tr_ref), custom_call_target="tpu_custom_call" | custom-call | tf_op jit(solution)/shard_map/pallas_call | solution.py:480

commit v7 on v6

--- a/solution.py
+++ b/solution.py
@@ -15,7 +15,7 @@
 UP, DOWN = 1, -1
 
 
-def kernel(n_row, n_col, n_layer, cols_ref, signs_ref, blk_ref, out_ref, tr_ref, own, left, right, high, low, acc,
+def kernel(n_row, n_col, n_layer, cols_ref, signs_ref, blk_ref, out_ref, tr_ref, own, left, right, split, acc_a, acc_b,
            flip, zero, mine, tb0, tb1, tb2, tb3, gsend, grecv, hsend, hrecv, osend, orecv, zsem, t0s, t0r, t1s, t1r, t2s, t2r,
            t3s, t3r):
     row, col, layer = lax.axis_index("row"), lax.axis_index("col"), lax.axis_index("layer")
@@ -184,9 +184,9 @@
 
     def put(r, k, x):
         h = x.astype(jnp.bfloat16)
-        lo = (x - h.astype(jnp.float32)).astype(jnp.bfloat16)
-        high[(r + 2) * B:(r + 3) * B, (k + 4) * B:(k + 5) * B] = h
-        low[(r + 2) * B:(r + 3) * B, (k + 4) * B:(k + 5) * B] = lo
+        at = ((r + 2) // 2 * 4 + r % 2) * B
+        split[at:at + B, (k + 4) * B:(k + 5) * B] = h
+        split[at + 2 * B:at + 3 * B, (k + 4) * B:(k + 5) * B] = (x - h.astype(jnp.float32)).astype(jnp.bfloat16)
 
     def put_both(r, k, x):
         if -2 <= r < 4:
@@ -197,14 +197,20 @@
     def product(tile, start, stop):
         i, j = CORNER[tile]
 
-        def part(ref, r):
-            return ref[(r + 2) * B:(r + 4) * B, (start + 4) * B:(stop + 4) * B]
+        def part(r, first, last):
+            at = (r + 2) * 2 * B
+            return split[at + first * B:at + last * B, (start + 4) * B:(stop + 4) * B]
 
         def dot(x, y):
             return lax.dot_general(x, y, (((1,), (1,)), ((), ())), preferred_element_type=jnp.float32)
 
-        ah, al, bh, bl = part(high, i), part(low, i), part(high, j), part(low, j)
-        return dot(ah, bh) + (dot(al, bh) + dot(ah, bl))
+        both = dot(part(i, 0, 4), part(j, 0, 2))
+        if tile == "A":
+            return both
+        return both[:2 * B] + (both[2 * B:] + dot(part(i, 0, 2), part(j, 2, 4)))
+
+    def whole(both):
+        return both[:2 * B] + (both[2 * B:] + both[2 * B:].T)
 
     def there(a, q):
         at_row = ROWS * (row * n_col + col) + 2 * b + a
@@ -330,8 +336,11 @@
             pl.when(t == 2)(share)
             for n, (a, q) in enumerate(BLOCKS):
                 put_both(a, q, own[t, n])
-            acc[0] = product("A", 0, 4)
-            acc[1] = product("B", 0, 2)
+            def within():
+                acc_a[...] = product("A", 0, 4)
+                acc_b[...] = product("B", 0, 2)
+
+            pl.when(t > 0)(within)
 
             def send(when, *copies):
                 @pl.when(when)
@@ -351,12 +360,13 @@
 
             come("B", UP, t)
             pl.when(t != 1)(lambda: make_d(True))
+            pl.when(t == 0)(within)
             def make_a():
-                finish(t, "A", acc[0] + product("A", -4, 0) + product("A", 4, 6), masks)
+                finish(t, "A", whole(acc_a[...] + product("A", -4, 0) + product("A", 4, 6)), masks)
 
             def make_b():
                 come("B", DOWN, t)
-                finish(t, "B", acc[1] + product("B", -2, 0) + product("B", 2, 6), masks)
+                finish(t, "B", acc_b[...] + product("B", -2, 0) + product("B", 2, 6), masks)
 
             come("D", DOWN, t)
 
@@ -446,9 +456,9 @@
                 pltpu.VMEM((STEPS + 1, 10, B, B), f32),
                 pltpu.VMEM((STEPS, 10, B, B), f32),
                 pltpu.VMEM((STEPS, 10, B, B), f32),
-                pltpu.VMEM((6 * B, 10 * B), bf16),
-                pltpu.VMEM((6 * B, 10 * B), bf16),
-                pltpu.VMEM((2, 2 * B, 2 * B), f32),
+                pltpu.VMEM((12 * B, 10 * B), bf16),
+                pltpu.VMEM((4 * B, 2 * B), f32),
+                pltpu.VMEM((2 * B, 2 * B), f32),
                 pltpu.VMEM((10, B, B), f32),
                 pltpu.VMEM((B, B), f32),
                 pltpu.VMEM((8, B), f32),

time: 55.2 us -> 54.9 us (level)
  no operation moved by 1% of the time
where the time goes in v7:
time: 54.9 us; the launch traced here: 54.1 us
  Pallas kernels  53.5 us (97%)
  between operations  0.64 us (1%)
    pallas_call x1, Pallas kernels, shards(): pl.pallas_call(body, out_shape=(jax.ShapeDtypeStruct(blocks.shape, f32),...  51.7 us
    pallas_call x1, Pallas kernels, shards(): pl.pallas_call(hand_over, grid=(2,), out_shape=(jax.ShapeDtypeStruct(bloc...  1.78 us

profile of v7, /device:TPU:1, one launch (start us, length us, event | category | flops | bytes accessed | tf_op | source)
XLA Modules:
  0.0 54.1 jit_solution(12512263384262426004)
XLA Ops:
  0.6 51.7 %shard_map.50 = (f32[4,2,128,128]{3,2,1,0:T(8,128)}, f32[3]{0:T(128)}) custom-call(s32[16,128]{1,0:T(8,128)} %bitcast.1, s32[3]{0:T(128)} %refs_1_.1, f32[4,2,128,128]{3,2,1,0:T(8,128)} %refs_2_.1), custom_call_target="tpu_custom_call" | custom-call | tf_op jit(solution)/shard_map/pallas_call | solution.py:446
  52.3 1.8 %shard_map.51 = (f32[4,2,128,128]{3,2,1,0:T(8,128)}, f32[3]{0:T(128)}) custom-call(f32[4,2,128,128]{3,2,1,0:T(8,128)} %get-tuple-element.4.out_ref, f32[3]{0:T(128)} %get-tuple-element.5.tr_ref), custom_call_target="tpu_custom_call" | custom-call | tf_op jit(solution)/shard_map/pallas_call | solution.py:490

commit v8 on v7

--- a/solution.py
+++ b/solution.py
@@ -92,26 +92,6 @@
     def _():
         greet((*here, 0))
 
-    @pl.when(collector)
-    def _():
-        for to in peer.values():
-            greet(to)
-        pl.semaphore_wait(barrier, 2 + (n_layer - 1) + n_layer + 2)
-
-    @pl.when(adder)
-    def _():
-        for to in [*col_peers, *row_peers]:
-            greet(to)
-        pl.semaphore_wait(barrier, 3 + (n_layer - 1) + (n_col - 1) + (n_row - 1))
-
-    @pl.when(jnp.logical_not(collector | adder) & (u < 6))
-    def _():
-        pl.semaphore_wait(barrier, 3)
-
-    @pl.when(u >= 6)
-    def _():
-        pl.semaphore_wait(barrier, 4)
-
     def sources(a):
         pair, d, q = a // 2, u - a, u - 2 * (a // 2)
         two, four = jnp.where(q >= 2, 1, 0), jnp.where(q >= 4, 1, 0)
@@ -130,6 +110,26 @@
         yield has, block, right.at[0, n], grecv.at[2, n], (*down, far + 1 + 2 * pair), False
 
     plans = list(zip(*(sources(a) for a in range(ROWS))))
+    @pl.when(collector)
+    def _():
+        for to in peer.values():
+            greet(to)
+        pl.semaphore_wait(barrier, 2 + (n_layer - 1) + n_layer + 2)
+
+    @pl.when(adder)
+    def _():
+        for to in [*col_peers, *row_peers]:
+            greet(to)
+        pl.semaphore_wait(barrier, 3 + (n_layer - 1) + (n_col - 1) + (n_row - 1))
+
+    @pl.when(jnp.logical_not(collector | adder) & (u < 6))
+    def _():
+        pl.semaphore_wait(barrier, 3)
+
+    @pl.when(u >= 6)
+    def _():
+        pl.semaphore_wait(barrier, 4)
+
     for k, plan in enumerate(plans):
         for a, (has, block, dst, sem, to, local) in enumerate(plan):
             @pl.when(has & jnp.logical_not(local))

time: 54.9 us -> 54.9 us (level)
  no operation moved by 1% of the time
where the time goes in v8:
time: 54.9 us; the launch traced here: 54.1 us
  Pallas kernels  53.5 us (97%)
  between operations  0.64 us (1%)
    pallas_call x1, Pallas kernels, shards(): pl.pallas_call(body, out_shape=(jax.ShapeDtypeStruct(blocks.shape, f32),...  51.7 us
    pallas_call x1, Pallas kernels, shards(): pl.pallas_call(hand_over, grid=(2,), out_shape=(jax.ShapeDtypeStruct(bloc...  1.78 us

profile of v8, /device:TPU:1, one launch (start us, length us, event | category | flops | bytes accessed | tf_op | source)
XLA Modules:
  0.0 54.1 jit_solution(2798031852685639762)
XLA Ops:
  0.6 51.7 %shard_map.50 = (f32[4,2,128,128]{3,2,1,0:T(8,128)}, f32[3]{0:T(128)}) custom-call(s32[16,128]{1,0:T(8,128)} %bitcast.1, s32[3]{0:T(128)} %refs_1_.1, f32[4,2,128,128]{3,2,1,0:T(8,128)} %refs_2_.1), custom_call_target="tpu_custom_call" | custom-call | tf_op jit(solution)/shard_map/pallas_call | solution.py:446
  52.3 1.8 %shard_map.51 = (f32[4,2,128,128]{3,2,1,0:T(8,128)}, f32[3]{0:T(128)}) custom-call(f32[4,2,128,128]{3,2,1,0:T(8,128)} %get-tuple-element.4.out_ref, f32[3]{0:T(128)} %get-tuple-element.5.tr_ref), custom_call_target="tpu_custom_call" | custom-call | tf_op jit(solution)/shard_map/pallas_call | solution.py:490

commit v9 on v8

--- a/solution.py
+++ b/solution.py
@@ -242,22 +242,17 @@
                 group = pick(b == 0, down, here)
                 r = jnp.where(b == 0, ROWS + a, 2 + a)
                 slot = jnp.where(b == 0, slot_up_before, slot_up) if wide else 0
-            yield own.at[STEPS, n], out_ref.at[r, slot], osend.at[0, n], orecv.at[r, slot], (*group, at_q), q == 1
+            yield None, (own.at[STEPS, n], out_ref.at[r, slot], osend.at[0, n], orecv.at[r, slot], (*group, at_q), q == 1)
             if q > a:
                 over = 2 * b + q >= ROWS
                 group = pick(over, up, here)
                 r = jnp.where(over, 2 * b + q - ROWS, 2 * b + q)
                 slot = jnp.where(over, slot_down_after, slot_down) if wide else 0
                 local = b == 0 if a == 1 else False
-                yield flip.at[n], out_ref.at[r, slot], osend.at[1, n], orecv.at[r, slot], (*group, at_a), local
+                yield n, (flip.at[n], out_ref.at[r, slot], osend.at[1, n], orecv.at[r, slot], (*group, at_a), local)
 
     def deliver(tile):
-        start, size = SPAN[tile]
-        for n in range(start, start + size):
-            a, q = BLOCKS[n]
-            if q > a:
-                flip[n] = own[STEPS, n].T
-        for src, dst, send, recv, to, local in results(tile):
+        def start(src, dst, send, recv, to, local):
             if local is not True:
                 @pl.when(jnp.logical_not(local))
                 def _():
@@ -267,8 +262,17 @@
                 def _():
                     pltpu.make_async_copy(src, dst, recv).start()
 
+        plan = list(results(tile))
+        for turned, result in plan:
+            if turned is None:
+                start(*result)
+        for turned, result in plan:
+            if turned is not None:
+                flip[turned] = own[STEPS, turned].T
+                start(*result)
+
     def delivered(tile):
-        for src, dst, send, recv, to, local in results(tile):
+        for _, (src, dst, send, recv, to, local) in results(tile):
             if local is not True:
                 @pl.when(jnp.logical_not(local))
                 def _():

time: 54.9 us -> 54.9 us (level)
  no operation moved by 1% of the time
where the time goes in v9:
time: 54.9 us; the launch traced here: 54.1 us
  Pallas kernels  53.5 us (97%)
  between operations  0.64 us (1%)
    pallas_call x1, Pallas kernels, shards(): pl.pallas_call(body, out_shape=(jax.ShapeDtypeStruct(blocks.shape, f32),...  51.7 us
    pallas_call x1, Pallas kernels, shards(): pl.pallas_call(hand_over, grid=(2,), out_shape=(jax.ShapeDtypeStruct(bloc...  1.78 us

profile of v9, /device:TPU:1, one launch (start us, length us, event | category | flops | bytes accessed | tf_op | source)
XLA Modules:
  0.0 54.1 jit_solution(13102694614721412492)
XLA Ops:
  0.6 51.7 %shard_map.50 = (f32[4,2,128,128]{3,2,1,0:T(8,128)}, f32[3]{0:T(128)}) custom-call(s32[16,128]{1,0:T(8,128)} %bitcast.1, s32[3]{0:T(128)} %refs_1_.1, f32[4,2,128,128]{3,2,1,0:T(8,128)} %refs_2_.1), custom_call_target="tpu_custom_call" | custom-call | tf_op jit(solution)/shard_map/pallas_call | solution.py:450
  52.3 1.8 %shard_map.51 = (f32[4,2,128,128]{3,2,1,0:T(8,128)}, f32[3]{0:T(128)}) custom-call(f32[4,2,128,128]{3,2,1,0:T(8,128)} %get-tuple-element.4.out_ref, f32[3]{0:T(128)} %get-tuple-element.5.tr_ref), custom_call_target="tpu_custom_call" | custom-call | tf_op jit(solution)/shard_map/pallas_call | solution.py:494
